TPU v7x, 128 devices: a whole 4x4x4 slice. The times are simulated.
128 devices in a mesh: dp: 16 (over z_lo, x, core), tensor: 8 (over y, z_hi).
Axes of the slice: x: 4, y: 4, z: 4 (z_hi: 2, z_lo: 2; z = z_hi * 2 + z_lo), core: 2. Of those that a mesh axis runs over, the one named last changes fastest.
Arguments:
- block_input: bfloat16 [512, 8192], P('tensor', 'dp'), may hold values from -24 to 24
- cotangent: bfloat16 [512, 8192], P('tensor', 'dp'), may hold values from -6 to 6
- attn_gain: float32 [8192], P('dp'), may hold values from 0.1 to 1.9
- attn_bias: float32 [8192], P('dp'), may hold values from -3 to 3
- mlp_gain: float32 [8192], P('dp'), may hold values from 0.1 to 1.9
- mlp_bias: float32 [8192], P('dp'), may hold values from -3 to 3
- w_qkv: bfloat16 [8192, 9216], P('dp', 'tensor'), may hold values from -0.0625 to 0.0625
- w_out: bfloat16 [8192, 8192], P('tensor', 'dp'), may hold values from -0.0625 to 0.0625
- w_up: bfloat16 [8192, 32768], P('dp', 'tensor'), may hold values from -0.0625 to 0.0625
- w_down: bfloat16 [32768, 8192], P('tensor', 'dp'), may hold values from -0.03125 to 0.03125
Outputs:
- input_grad: bfloat16 [512, 8192], P('tensor', 'dp')
- norm_grads: float32 [4, 8192], P(None, 'dp')
- grad_qkv: bfloat16 [8192, 9216], P('dp', 'tensor')
- grad_out: bfloat16 [8192, 8192], P('tensor', 'dp')
- grad_up: bfloat16 [8192, 32768], P('dp', 'tensor')
- grad_down: bfloat16 [32768, 8192], P('tensor', 'dp')
All inputs are finite; a program needn't handle non-finite values.
Results may differ from a plain program's by a relative error of at most 0.03.
Values may be sent and summed in bfloat16 or wider, within the bound.
A program may use at most 128 MiB of HBM per device.

v0:
```python
import math

import jax
import jax.numpy as jnp
from jax import lax
from jax.sharding import PartitionSpec as P

D = 8192
HEADS = 128
G = 8
HD = 64
LENGTH = 512


def gelu_value(argument):
    return 0.5 * argument * (1.0 + lax.erf(argument * 0.7071067811865476))


def gelu_slope(argument):
    return (
        0.5 * (1.0 + lax.erf(argument * 0.7071067811865476))
        + argument * jnp.exp(-0.5 * argument * argument) * 0.3989422804014327
    )


def rope_columns(tokens):
    halfway = HD // 2
    position = (jnp.arange(tokens) % LENGTH).astype(jnp.float32)
    frequency = 10000.0 ** (-2.0 * jnp.arange(halfway).astype(jnp.float32) / HD)
    angle = frequency[:, None] * position[None, :]
    cosine = jnp.concatenate([jnp.cos(angle), jnp.cos(angle)], 0)
    sine = jnp.concatenate([jnp.sin(angle), jnp.sin(angle)], 0)
    return (cosine, sine)


def rotate_rows(values, cosine, sine):
    halfway = values.shape[-2] // 2
    turned = jnp.concatenate([-values[..., halfway:, :], values[..., :halfway, :]], -2)
    return values * cosine + turned * sine


def unrotate_rows(values, cosine, sine):
    halfway = values.shape[-2] // 2
    scaled = values * sine
    back = jnp.concatenate([scaled[..., halfway:, :], -scaled[..., :halfway, :]], -2)
    return values * cosine + back


def across_tokens(weights, token_major):
    return lax.dot_general(
        weights, token_major, (((0,), (1,)), ((), ())), preferred_element_type=jnp.float32
    )


def rows_by_tokens(weights, token_major):
    return lax.dot_general(
        weights, token_major, (((1,), (1,)), ((), ())), preferred_element_type=jnp.float32
    )


def attend(queries, keys_mine, values_mine, out_grad):
    head_count, head_dim, tokens = queries.shape
    seqcount = tokens // LENGTH
    scaling = 1.0 / math.sqrt(head_dim)
    shaped_q = queries.reshape(head_count, head_dim, seqcount, LENGTH)
    shaped_k = keys_mine.reshape(head_dim, seqcount, LENGTH)
    shaped_v = values_mine.reshape(head_dim, seqcount, LENGTH)
    shaped_g = out_grad.reshape(head_count, head_dim, seqcount, LENGTH)
    scores = (
        jnp.einsum("hdsn,dsm->hsnm", shaped_q, shaped_k, preferred_element_type=jnp.float32)
        * scaling
    )
    causal = lax.broadcasted_iota(jnp.int32, (LENGTH, LENGTH), 0) >= lax.broadcasted_iota(
        jnp.int32, (LENGTH, LENGTH), 1
    )
    raised = jnp.where(causal, jnp.exp(scores), 0.0)
    probability = raised / jnp.sum(raised, -1, keepdims=True)
    prob_low = probability.astype(jnp.bfloat16)
    outputs = jnp.einsum(
        "hsnm,dsm->hdsn", prob_low, shaped_v, preferred_element_type=jnp.float32
    ).astype(jnp.bfloat16)
    dropped = jnp.einsum("hdsn,dsm->hsnm", shaped_g, shaped_v, preferred_element_type=jnp.float32)
    row_dot = jnp.einsum("hdsn,hdsn->hsn", shaped_g, outputs, preferred_element_type=jnp.float32)
    score_grad = (probability * (dropped - row_dot[..., None]) * scaling).astype(jnp.bfloat16)
    query_grad = jnp.einsum(
        "hsnm,dsm->hdsn", score_grad, shaped_k, preferred_element_type=jnp.float32
    )
    key_grad = jnp.einsum(
        "hsnm,hdsn->dsm", score_grad, shaped_q, preferred_element_type=jnp.float32
    )
    value_grad = jnp.einsum(
        "hsnm,hdsn->dsm", prob_low, shaped_g, preferred_element_type=jnp.float32
    )
    return (
        outputs.reshape(head_count, head_dim, tokens),
        query_grad.reshape(head_count, head_dim, tokens),
        key_grad.reshape(head_dim, tokens),
        value_grad.reshape(head_dim, tokens),
    )


def on_device(
    block_input, cotangent, attn_gain, attn_bias, mlp_gain, mlp_bias, w_qkv, w_out, w_up, w_down
):
    per_group = HEADS // G
    inputs = block_input.astype(jnp.float32)
    totals = lax.psum((jnp.sum(inputs, 1), jnp.sum(inputs * inputs, 1)), "dp")
    average = totals[0] / D
    spread = totals[1] / D - average * average
    inverse = lax.rsqrt(spread + 1e-05)
    normed = (inputs - average[:, None]) * inverse[:, None]
    attn_local = (normed * attn_gain + attn_bias).astype(jnp.bfloat16)
    mlp_local = (normed * mlp_gain + mlp_bias).astype(jnp.bfloat16)
    attn_in, mlp_in, grad_in = (
        lax.all_gather(attn_local, "tensor", axis=0, tiled=True),
        lax.all_gather(mlp_local, "tensor", axis=0, tiled=True),
        lax.all_gather(cotangent, "tensor", axis=0, tiled=True),
    )
    tokens = attn_in.shape[0]
    width_local = attn_in.shape[1]
    groups = w_qkv.shape[1] // ((per_group + 2) * HD)
    dp_count = lax.axis_size("dp")
    dp_index = lax.axis_index("dp")
    my_heads = groups * per_group // dp_count
    my_rows = my_heads * HD
    my_group = dp_index * my_heads // per_group
    split_weight = w_qkv.reshape(width_local, groups, per_group + 2, HD)
    query_weight = split_weight[:, :, :per_group].reshape(width_local, groups * per_group * HD)
    pair_weight = split_weight[:, :, per_group:].reshape(width_local, groups * 2 * HD)
    whole_sum = lax.psum(across_tokens(w_qkv, attn_in), "dp").reshape(
        groups, per_group + 2, HD, tokens
    )
    query_all = whole_sum[:, :per_group].reshape(groups * per_group * HD, tokens)
    query_sum = lax.dynamic_slice_in_dim(query_all, dp_index * my_rows, my_rows, 0)
    pair_sum = whole_sum[:, per_group:].reshape(groups * 2 * HD, tokens)
    cosine, sine = rope_columns(tokens)
    pair_mine = lax.dynamic_index_in_dim(
        pair_sum.reshape(groups, 2, HD, tokens), my_group, 0, keepdims=False
    )
    queries = rotate_rows(query_sum.reshape(my_heads, HD, tokens), cosine, sine).astype(
        jnp.bfloat16
    )
    keys_mine = rotate_rows(pair_mine[0], cosine, sine).astype(jnp.bfloat16)
    values_mine = pair_mine[1].astype(jnp.bfloat16)
    out_grad = lax.psum_scatter(
        rows_by_tokens(w_out, grad_in).astype(jnp.bfloat16), "dp", scatter_dimension=0, tiled=True
    )
    head_out, query_grad, key_grad, value_grad = attend(
        queries, keys_mine, values_mine, out_grad.reshape(my_heads, HD, tokens)
    )
    grad_out = jnp.dot(
        lax.all_gather(head_out.reshape(my_rows, tokens), "dp", axis=0, tiled=True),
        grad_in,
        preferred_element_type=jnp.float32,
    ).astype(jnp.bfloat16)
    query_low = (
        unrotate_rows(query_grad, cosine, sine).astype(jnp.bfloat16).reshape(my_rows, tokens)
    )
    pair_part = jnp.zeros((groups, 2, HD, tokens), jnp.float32)
    pair_part = lax.dynamic_update_index_in_dim(
        pair_part, jnp.stack([key_grad, value_grad]), my_group, 0
    )
    pair_total = lax.psum(pair_part.astype(jnp.bfloat16), "dp").astype(jnp.float32)
    pair_low = jnp.stack([unrotate_rows(pair_total[:, 0], cosine, sine), pair_total[:, 1]], 1)
    pair_low = pair_low.astype(jnp.bfloat16).reshape(groups * 2 * HD, tokens)
    pair_back = across_tokens(pair_low, pair_weight)
    pair_grad_w = across_tokens(attn_in, pair_low)
    fragment = lax.all_gather(query_low, "dp", axis=0, tiled=True)
    back_part = pair_back
    weight_part = across_tokens(attn_in, fragment)
    back_part = back_part + across_tokens(fragment, query_weight)
    query_grad_w = weight_part
    attn_back = back_part
    grad_qkv = jnp.concatenate(
        [
            query_grad_w.reshape(width_local, groups, per_group * HD),
            pair_grad_w.reshape(width_local, groups, 2 * HD),
        ],
        2,
    )
    grad_qkv = grad_qkv.reshape(width_local, groups * (per_group + 2) * HD).astype(jnp.bfloat16)
    hidden = lax.psum_scatter(
        across_tokens(w_up, mlp_in).astype(jnp.bfloat16), "dp", scatter_dimension=0, tiled=True
    ).astype(jnp.float32)
    grad_down = jnp.dot(
        lax.all_gather(gelu_value(hidden).astype(jnp.bfloat16), "dp", axis=0, tiled=True),
        grad_in,
        preferred_element_type=jnp.float32,
    ).astype(jnp.bfloat16)
    hidden_grad = (
        lax.psum_scatter(
            rows_by_tokens(w_down, grad_in).astype(jnp.bfloat16),
            "dp",
            scatter_dimension=0,
            tiled=True,
        ).astype(jnp.float32)
        * gelu_slope(hidden)
    ).astype(jnp.bfloat16)
    fragment = lax.all_gather(hidden_grad, "dp", axis=0, tiled=True)
    weight_part = across_tokens(mlp_in, fragment)
    back_part = across_tokens(fragment, w_up)
    grad_up = weight_part.astype(jnp.bfloat16)
    attn_share, mlp_share = (
        lax.psum_scatter(
            attn_back.astype(jnp.bfloat16), "tensor", scatter_dimension=0, tiled=True
        ).astype(jnp.float32),
        lax.psum_scatter(
            back_part.astype(jnp.bfloat16), "tensor", scatter_dimension=0, tiled=True
        ).astype(jnp.float32),
    )
    normed_grad = attn_share * attn_gain + mlp_share * mlp_gain
    moments = lax.psum((jnp.sum(normed_grad, 1), jnp.sum(normed_grad * normed, 1)), "dp")
    first = moments[0] / D
    second = moments[1] / D
    input_grad = (
        cotangent.astype(jnp.float32)
        + inverse[:, None] * (normed_grad - first[:, None] - normed * second[:, None])
    ).astype(jnp.bfloat16)
    local_norm = jnp.stack(
        [
            jnp.sum(attn_share * normed, 0),
            jnp.sum(attn_share, 0),
            jnp.sum(mlp_share * normed, 0),
            jnp.sum(mlp_share, 0),
        ]
    )
    norm_grads = lax.psum(local_norm, "tensor")
    return (input_grad, norm_grads, grad_qkv, grad_out, grad_up, grad_down)


def solution(mesh):
    return jax.shard_map(
        on_device,
        mesh=mesh,
        in_specs=(
            P("tensor", "dp"),
            P("tensor", "dp"),
            P("dp"),
            P("dp"),
            P("dp"),
            P("dp"),
            P("dp", "tensor"),
            P("tensor", "dp"),
            P("dp", "tensor"),
            P("tensor", "dp"),
        ),
        out_specs=(
            P("tensor", "dp"),
            P(None, "dp"),
            P("dp", "tensor"),
            P("tensor", "dp"),
            P("dp", "tensor"),
            P("tensor", "dp"),
        ),
        check_vma=False,
    )
```

profile of v0, /device:TPU:1, one launch (start us, length us, event | category | flops | bytes accessed | tf_op | source)
XLA Modules:
  0.0 881.5 jit_solution(5248890537811261545)
XLA Ops:
  7.2 1.0 fusion.27
  8.3 28.4 %all-reduce.1 = (f32[64]{0:T(128)S(1)}, f32[64]{0:T(128)S(1)}) all-reduce(f32[64]{0:T(128)S(1)} %get-tuple-element.13, f32[64]{0:T(128)S(1)} %get-tuple-element.12), channel_id=1, replica_groups=mesh['dp'=16,'tensor'=8] {'dp'}, use_global_device_ids=true, to_apply=%region_3.0 | all-reduce | flops 128 | bytes 1024 | tf_op jit(solution)/shard_map/psum | solution.py:107
  36.7 1.0 fusion.34
  37.6 29.6 %all_gather.21 = bf16[512,512]{1,0:T(8,128)(2,1)S(1)} all-gather(bf16[64,512]{1,0:T(8,128)(2,1)S(1)} %get-tuple-element.28), channel_id=1, replica_groups=mesh['dp'=16,'tensor'=8] {'tensor'}, dimensions={0}, use_global_device_ids=true | all-gather | bytes 589824 | tf_op jit(solution)/shard_map/all_gather | solution.py:115
  67.3 0.8 copy-done.1
  68.1 2.1 convolution_bitcast_fusion
  70.2 2.0 copy.20
  72.3 29.3 %all_gather.22 = bf16[512,512]{1,0:T(8,128)(2,1)S(1)} all-gather(bf16[64,512]{1,0:T(8,128)(2,1)S(1)} %copy-done.9), channel_id=1, replica_groups=mesh['dp'=16,'tensor'=8] {'tensor'}, dimensions={0}, use_global_device_ids=true | all-gather | bytes 589824 | tf_op jit(solution)/shard_map/all_gather | solution.py:117
  101.6 1.7 convolution_convert_fusion.6
  103.4 29.0 %all_gather.24 = bf16[512,512]{1,0:T(8,128)(2,1)S(1)} all-gather(bf16[64,512]{1,0:T(8,128)(2,1)S(1)} %get-tuple-element.29), channel_id=1, replica_groups=mesh['dp'=16,'tensor'=8] {'tensor'}, dimensions={0}, use_global_device_ids=true | all-gather | bytes 589824 | tf_op jit(solution)/shard_map/all_gather | solution.py:116
  132.4 0.8 copy-done.6
  133.2 6.6 fusion
  140.0 6.6 convolution_convert_fusion.3
  147.3 58.6 %all-reduce.5.cloned.1.call-done = f32[1,18,64,512]{3,2,1,0:T(8,128)} async-done(((f32[1,18,64,512]{3,2,1,0:T(8,128)}), f32[1,18,64,512]{3,2,1,0:T(8,128)}) %all-reduce.5.cloned.1.call-update) | async-done | bytes 2359312 | tf_op jit(solution)/shard_map/psum | solution.py:130
  205.9 1.8 slice.70
  207.8 0.9 slice_negate_fusion.2
  208.7 0.9 fusion.46
  210.4 57.5 %reduce-scatter.6.cloned.1.call-done = bf16[64,512]{1,0:T(8,128)(2,1)} async-done(((bf16[1024,512]{1,0:T(8,128)(2,1)}), bf16[64,512]{1,0:T(8,128)(2,1)}) %reduce-scatter.6.cloned.1.call-update) | async-done | bytes 65552 | tf_op jit(solution)/shard_map/reduce_scatter | solution.py:145
  267.8 1.8 fusion.61
  269.6 1.2 fusion.11
  272.1 1.0 fusion.67
  274.7 61.3 %reduce-scatter.12.cloned.1.call-done = bf16[256,512]{1,0:T(8,128)(2,1)} async-done(((bf16[4096,512]{1,0:T(8,128)(2,1)}), bf16[256,512]{1,0:T(8,128)(2,1)}) %reduce-scatter.12.cloned.1.call-update) | async-done | bytes 262160 | tf_op jit(solution)/shard_map/reduce_scatter | solution.py:182
  336.1 68.3 %reduce-scatter.10.cloned.1.call-done = bf16[256,512]{1,0:T(8,128)(2,1)} async-done(((bf16[4096,512]{1,0:T(8,128)(2,1)}), bf16[256,512]{1,0:T(8,128)(2,1)}) %reduce-scatter.10.cloned.1.call-update) | async-done | bytes 262160 | tf_op jit(solution)/shard_map/reduce_scatter | solution.py:191
  404.3 2.1 fusion.23
  407.3 1.6 copy.21
  408.8 1.1 slice.84
  409.9 115.3 %all-reduce.7.cloned.1.call-done = bf16[1,2,64,512]{3,2,1,0:T(8,128)(2,1)} async-done(((bf16[1,2,64,512]{3,2,1,0:T(8,128)(2,1)}), bf16[1,2,64,512]{3,2,1,0:T(8,128)(2,1)}) %all-reduce.7.cloned.1.call-update) | async-done | bytes 131088 | tf_op jit(solution)/shard_map/psum | solution.py:163
  525.2 0.9 convert_element_type.185
  526.2 0.8 slice.113
  527.1 0.8 slice_bitcast_fusion.5
  528.0 1.3 convolution_bitcast_fusion.1
  529.6 31.1 %all-gather.5.cloned.1.call-done = bf16[1024,512]{1,0:T(8,128)(2,1)} async-done(((bf16[64,512]{1,0:T(8,128)(2,1)}), bf16[1024,512]{1,0:T(8,128)(2,1)}) %all-gather.5.cloned.1.call-update) | async-done | bytes 1048592 | tf_op jit(solution)/shard_map/all_gather | solution.py:168
  560.8 3.5 fusion.8
  564.5 0.8 fusion.3
  565.3 1.1 maximum_bitcast_fusion
  566.4 29.2 %all-gather.9.cloned.1.call-done = bf16[1024,512]{1,0:T(8,128)(2,1)} async-done(((bf16[64,512]{1,0:T(8,128)(2,1)}), bf16[1024,512]{1,0:T(8,128)(2,1)}) %all-gather.9.cloned.1.call-update) | async-done | bytes 1048592 | tf_op jit(solution)/shard_map/all_gather | solution.py:152
  595.6 2.9 convolution_convert_fusion.4
  598.5 36.9 %all-gather.7.cloned.1.call-done = bf16[4096,512]{1,0:T(8,128)(2,1)} async-done(((bf16[256,512]{1,0:T(8,128)(2,1)}), bf16[4096,512]{1,0:T(8,128)(2,1)}) %all-gather.7.cloned.1.call-update) | async-done | bytes 4194320 | tf_op jit(solution)/shard_map/all_gather | solution.py:199
  635.4 6.6 convolution_convert_fusion.7
  642.1 6.6 convolution_convert_fusion.1
  648.7 26.5 %all-gather.11.cloned.1.call-done = bf16[4096,512]{1,0:T(8,128)(2,1)} async-done(((bf16[256,512]{1,0:T(8,128)(2,1)}), bf16[4096,512]{1,0:T(8,128)(2,1)}) %all-gather.11.cloned.1.call-update) | async-done | bytes 4194320 | tf_op jit(solution)/shard_map/all_gather | solution.py:186
  675.1 6.5 convolution_convert_fusion
  681.7 65.4 %reduce-scatter.8.cloned.1.call-done = bf16[64,512]{1,0:T(8,128)(2,1)} async-done(((bf16[512,512]{1,0:T(8,128)(2,1)}), bf16[64,512]{1,0:T(8,128)(2,1)}) %reduce-scatter.8.cloned.1.call-update) | async-done | bytes 65552 | tf_op jit(solution)/shard_map/reduce_scatter | solution.py:204
  747.0 73.8 %reduce-scatter.14.cloned.1.call-done = bf16[64,512]{1,0:T(8,128)(2,1)} async-done(((bf16[512,512]{1,0:T(8,128)(2,1)}), bf16[64,512]{1,0:T(8,128)(2,1)}) %reduce-scatter.14.cloned.1.call-update) | async-done | bytes 65552 | tf_op jit(solution)/shard_map/reduce_scatter | solution.py:207
  820.8 1.1 fusion.62
  821.9 18.7 %psum.55 = f32[4,512]{1,0:T(4,128)} all-reduce(f32[4,512]{1,0:T(4,128)S(1)} %pad_maximum_fusion.5), channel_id=1, replica_groups=mesh['dp'=16,'tensor'=8] {'tensor'}, use_global_device_ids=true, to_apply=%region_20.21 | all-reduce | flops 2048 | bytes 16384 | tf_op jit(solution)/shard_map/psum | solution.py:227
  840.6 32.8 %all-reduce = (f32[64]{0:T(128)S(1)}, f32[64]{0:T(128)S(1)}) all-reduce(f32[64]{0:T(128)S(1)} %get-tuple-element.7, f32[64]{0:T(128)S(1)} %get-tuple-element.6), channel_id=1, replica_groups=mesh['dp'=16,'tensor'=8] {'dp'}, use_global_device_ids=true, to_apply=%region_15.16 | all-reduce | flops 128 | bytes 1024 | tf_op jit(solution)/shard_map/psum | solution.py:212
  873.4 1.6 fusion.41
  (71 shorter events, 6.0 us)
Async XLA Ops:
  7.2 94.4 %copy-start = (bf16[1024,512]{1,0:T(8,128)(2,1)S(1)}, bf16[1024,512]{1,0:T(8,128)(2,1)}, u32[]{:S(2)}) copy-start(bf16[1024,512]{1,0:T(8,128)(2,1)} %param.17) | copy-start | bytes 3145732
  7.2 198.7 %all-reduce.5.cloned.1.call-start = ((), (), s32[]{:S(2)}) async-start(), calls=%async_computation.5 | async-start | bytes 4718592 | tf_op jit(solution)/shard_map/psum | solution.py:130
  67.3 0.8 copy-start.1
  70.2 2.1 copy-start.9
  72.2 195.6 %reduce-scatter.6.cloned.1.call-start = ((), (), s32[]{:S(2)}) async-start(), calls=%async_computation.6 | async-start | bytes 1114112 | tf_op jit(solution)/shard_map/reduce_scatter | solution.py:145
  101.6 38.3 %copy-start.4 = (bf16[512,512]{1,0:T(8,128)(2,1)}, bf16[512,512]{1,0:T(8,128)(2,1)S(1)}, u32[]{:S(2)}) copy-start(bf16[512,512]{1,0:T(8,128)(2,1)S(1)} %all_gather.22) | copy-start | bytes 1572868
  103.3 232.7 %reduce-scatter.12.cloned.1.call-start = ((), (), s32[]{:S(2)}) async-start(), calls=%async_computation.11 | async-start | bytes 4456448 | tf_op jit(solution)/shard_map/reduce_scatter | solution.py:182
  132.4 0.8 copy-start.6
  139.9 264.4 %reduce-scatter.10.cloned.1.call-start = ((), (), s32[]{:S(2)}) async-start(), calls=%async_computation.10 | async-start | bytes 4456448 | tf_op jit(solution)/shard_map/reduce_scatter | solution.py:191
  146.6 378.6 %all-reduce.7.cloned.1.call-start = ((), (), s32[]{:S(2)}) async-start(), calls=%async_computation.7 | async-start | bytes 262144 | tf_op jit(solution)/shard_map/psum | solution.py:163
  209.6 0.6 copy-start.10
  267.8 3.3 copy-start.8
  273.2 287.5 %all-gather.5.cloned.1.call-start = ((), (), s32[]{:S(2)}) async-start(), calls=%async_computation.8 | async-start | bytes 1114112 | tf_op jit(solution)/shard_map/all_gather | solution.py:168
  273.9 321.6 %all-gather.9.cloned.1.call-start = ((), (), s32[]{:S(2)}) async-start(), calls=%async_computation.14 | async-start | bytes 1114112 | tf_op jit(solution)/shard_map/all_gather | solution.py:152
  274.7 360.7 %all-gather.7.cloned.1.call-start = ((), (), s32[]{:S(2)}) async-start(), calls=%async_computation.12 | async-start | bytes 4456448 | tf_op jit(solution)/shard_map/all_gather | solution.py:199
  406.4 122.8 %copy-start.2 = (bf16[512,512]{1,0:T(8,128)(2,1)S(1)}, bf16[512,512]{1,0:T(8,128)(2,1)}, u32[]{:S(2)}) copy-start(bf16[512,512]{1,0:T(8,128)(2,1)} %copy-done.1) | copy-start | bytes 1572868
  406.5 268.7 %all-gather.11.cloned.1.call-start = ((), (), s32[]{:S(2)}) async-start(), calls=%async_computation.15 | async-start | bytes 4456448 | tf_op jit(solution)/shard_map/all_gather | solution.py:186
  407.2 339.8 %reduce-scatter.8.cloned.1.call-start = ((), (), s32[]{:S(2)}) async-start(), calls=%async_computation.9 | async-start | bytes 589824 | tf_op jit(solution)/shard_map/reduce_scatter | solution.py:204
  560.7 3.8 copy-start.13
  560.7 34.8 %copy-start.5 = (bf16[512,512]{1,0:T(8,128)(2,1)S(1)}, bf16[512,512]{1,0:T(8,128)(2,1)}, u32[]{:S(2)}) copy-start(bf16[512,512]{1,0:T(8,128)(2,1)} %copy-done.4) | copy-start | bytes 1572868
  564.3 256.5 %reduce-scatter.14.cloned.1.call-start = ((), (), s32[]{:S(2)}) async-start(), calls=%async_computation.13 | async-start | bytes 589824 | tf_op jit(solution)/shard_map/reduce_scatter | solution.py:207
  598.5 43.6 %copy-start.7 = (bf16[512,512]{1,0:T(8,128)(2,1)S(1)}, bf16[512,512]{1,0:T(8,128)(2,1)}, u32[]{:S(2)}) copy-start(bf16[512,512]{1,0:T(8,128)(2,1)} %copy-done.6) | copy-start | bytes 1572868
  648.7 172.1 %copy-start.3 = (bf16[64,512]{1,0:T(8,128)(2,1)S(1)}, bf16[64,512]{1,0:T(8,128)(2,1)}, u32[]{:S(2)}) copy-start(bf16[64,512]{1,0:T(8,128)(2,1)} %param.10) | copy-start | bytes 196612
  648.7 172.1 %copy-start.11 = (f32[512]{0:T(512)S(1)}, f32[512]{0:T(512)}, u32[]{:S(2)}) copy-start(f32[512]{0:T(512)} %param.12) | copy-start | bytes 6148
  648.7 172.1 %copy-start.12 = (f32[512]{0:T(512)S(1)}, f32[512]{0:T(512)}, u32[]{:S(2)}) copy-start(f32[512]{0:T(512)} %param.14) | copy-start | bytes 6148
Sparse Core Ops, SparseCore 0:
  72.3 133.5 all-reduce.4
  208.8 58.9 reduce-scatter.5
  271.0 65.0 reduce-scatter.11
  339.0 65.2 reduce-scatter.9
  407.4 117.8 all-reduce.6
  526.8 33.8 all-gather.4
  563.0 32.4 all-gather.8
  597.8 37.4 all-gather.6
  637.7 37.4 all-gather.10
  678.6 68.4 reduce-scatter.7
  751.1 69.7 reduce-scatter.13
where the time goes:
time: 882 us
  waiting for transfers between devices  625 us (71%)
  blocking collectives  168 us (19%)
  matrix products  50.6 us (6%)
  between operations  14.1 us (2%)
  other arithmetic  12.9 us (1%)
  local copies, waits for them, and re-layouts  10.1 us (1%)
    psum x1, waiting for transfers between devices, on_device(): lax.psum(pair_part.astype(jnp.bfloat16), 'dp').astype(jnp.float32)  115 us
    reduce_scatter x1, waiting for transfers between devices, on_device(): lax.psum_scatter(back_part.astype(jnp.bfloat16), 'tensor', scatter_dimens...  73.8 us
    reduce_scatter x1, waiting for transfers between devices, on_device(): lax.psum_scatter(rows_by_tokens(w_down, grad_in).astype(jnp.bfloat16), 'd...  68.3 us
    reduce_scatter x1, waiting for transfers between devices, on_device(): lax.psum_scatter(attn_back.astype(jnp.bfloat16), 'tensor', scatter_dimens...  65.4 us
    reduce_scatter x1, waiting for transfers between devices, on_device(): lax.psum_scatter(across_tokens(w_up, mlp_in).astype(jnp.bfloat16), 'dp',...  61.3 us
    psum x1, waiting for transfers between devices, on_device(): lax.psum(across_tokens(w_qkv, attn_in), 'dp')  58.6 us
    reduce_scatter x1, waiting for transfers between devices, on_device(): lax.psum_scatter(rows_by_tokens(w_out, grad_in).astype(jnp.bfloat16), 'dp...  57.5 us
    all_gather x1, waiting for transfers between devices, on_device(): fragment = lax.all_gather(hidden_grad, 'dp', axis=0, tiled=True)  36.9 us
  transfers between devices with their start and end apart: 11, of which 11 were waited for; matrix products, arithmetic and copies ran while one was open for 7% of the time, Pallas kernels for 0%

commit v1 on v0

v1 whole, which is shorter than its diff:
```python
import functools
import math

import jax
import jax.numpy as jnp
from jax import lax
from jax.experimental import pallas as pl
from jax.experimental.pallas import tpu as pltpu
from jax.sharding import PartitionSpec as P

D = 8192
HD = 64
LENGTH = 512
TOK = 512
W = 512
ROWS = 64
NT = 8
ND = 16
FF = 4096
CH = 256
QKV = 1152
MESH = pl.DeviceIdType.MESH
BF = jnp.bfloat16
F32 = jnp.float32


def dot_nn(a, b):
    return jnp.dot(a, b, preferred_element_type=F32)


def dot_nt(a, b):
    return lax.dot_general(a, b, (((1,), (1,)), ((), ())), preferred_element_type=F32)


def gelu_parts(v):
    half = 0.5 * (1.0 + lax.erf(v * 0.7071067811865476))
    return v * half, half + v * jnp.exp(-0.5 * v * v) * 0.3989422804014327


def rope_columns():
    halfway = HD // 2
    position = (jnp.arange(TOK) % LENGTH).astype(F32)
    frequency = 10000.0 ** (-2.0 * jnp.arange(halfway).astype(F32) / HD)
    angle = frequency[:, None] * position[None, :]
    cosine = jnp.concatenate([jnp.cos(angle), jnp.cos(angle)], 0)
    sine = jnp.concatenate([jnp.sin(angle), jnp.sin(angle)], 0)
    return cosine, sine


def rotate(v, cosine, sine):
    turned = jnp.concatenate([-v[32:], v[:32]], 0)
    return v * cosine + turned * sine


def unrotate(v, cosine, sine):
    scaled = v * sine
    back = jnp.concatenate([scaled[32:], -scaled[:32]], 0)
    return v * cosine + back


def kernel(
    x_loc, c_loc, ag, ab, mg, mb, cosine, sine, wq_hbm, wo_hbm, wu_hbm, wd_hbm,
    out_x, out_n, out_q, out_o, out_u, out_d,
    xs, cs, st_in, st, wq, wqt, wo, wu, wd, ain, min_, ain_t, min_t,
    pa, pkv, pa_in, pkv_in, sa, ra, kvx,
    pd_out, pd_in, od, rd, ph_out, ph_in, oh, rh,
    ah, hq, proj, pp, pp_in, psum, pr,
    abt, mbt, ngb, ngr, mom, momr, nrm, nrmr, m2,
    w_sem, x_s, x_r, c_s, c_r, st_s, st_r, tt_s, tt_r,
    a_sem, sa_s, sa_r, kv_sem,
    pd_s, pd_r, rd_s, rd_r, ph_s, ph_r, rh_s, rh_r,
    ah_s, ah_r, fa_s, fa_r, hq_s, hq_r, fh_s, fh_r, pp_sem, pr_s, pr_r, pj_sem,
    o_sem, u_sem, d_sem, ng_s, ng_r, mo_s, mo_r, nr_s, nr_r, m2_s, m2_r,
):
    d = lax.axis_index("dp")
    t = lax.axis_index("tensor")
    c = d % 2
    xx = (d // 2) % 4
    zl = d // 8
    other = 1 - c
    partner = (d + 1 - 2 * c, t)
    mine = d // 2

    def to_chip(s):
        return ((zl + s % 2) % 2) * 4 + (xx + s // 2) % 4

    def from_chip(s):
        return ((zl + s % 2) % 2) * 4 + (xx + 4 - s // 2) % 4

    def remote(src, dst, send, recv, device):
        return pltpu.make_async_remote_copy(
            src_ref=src, dst_ref=dst, send_sem=send, recv_sem=recv, device_id=device, device_id_type=MESH
        )

    def rows(index, size):
        return pl.ds(pl.multiple_of(index * size, size), size)

    weights = [
        pltpu.make_async_copy(src, dst, w_sem.at[i])
        for i, (src, dst) in enumerate([(wd_hbm, wd), (wq_hbm, wq), (wo_hbm, wo), (wu_hbm, wu)])
    ]
    for copy in weights:
        copy.start()

    barrier = pltpu.get_barrier_semaphore()

    def greet_t(k, carry):
        pl.semaphore_signal(barrier, inc=1, device_id=(d, (t + k) % NT), device_id_type=MESH)
        return carry

    def greet_d(k, carry):
        pl.semaphore_signal(barrier, inc=1, device_id=((d + k) % ND, t), device_id_type=MESH)
        return carry

    lax.fori_loop(1, NT, greet_t, 0)
    lax.fori_loop(1, ND, greet_d, 0)
    pl.semaphore_wait(barrier, NT - 1 + ND - 1)

    own = rows(t, ROWS)

    def send_c(k):
        return remote(c_loc, cs.at[own], c_s.at[k], c_r.at[k], (d, (t + k) % NT))

    def send_x(k):
        return remote(x_loc, xs.at[own], x_s.at[k], x_r.at[k], (d, (t + k) % NT))

    def start_gather(k, carry):
        send_c(k).start()
        send_x(k).start()
        return carry

    lax.fori_loop(1, NT, start_gather, 0)
    cs[own, :] = c_loc[...]
    xs[own, :] = x_loc[...]
    lane = lax.broadcasted_iota(jnp.int32, (ROWS, 128), 1)
    xf = x_loc[...].astype(F32)
    st_in[0] = jnp.where(
        lane < 64, jnp.sum(xf, 1, keepdims=True), jnp.sum(xf * xf, 1, keepdims=True)
    )

    def send_st(k):
        return remote(st_in.at[0], st_in.at[k], st_s.at[k], st_r.at[k], ((d + k) % ND, t))

    def send_tt(k):
        return remote(st.at[own], st.at[own], tt_s.at[k], tt_r.at[k], (d, (t + k) % NT))

    def loop(low, high, f):
        def body(k, carry):
            f(k)
            return carry

        lax.fori_loop(low, high, body, 0)

    loop(1, ND, lambda k: send_st(k).start())
    weights[1].wait()
    for i in range(QKV // 128):
        wqt[i * 128 : (i + 1) * 128, :] = wq[:, i * 128 : (i + 1) * 128].T
    loop(1, ND, lambda k: send_st(k).wait_recv())
    total = st_in[0]
    for k in range(1, ND):
        total = total + st_in[k]
    st[own, :] = total
    loop(1, NT, lambda k: send_tt(k).start())

    def pair_copy(out, into, send, recv, r):
        return remote(out.at[r], into.at[r], send.at[r], recv.at[r], partner)

    def chip_copy(buf, into, send, recv, r):
        return remote(buf.at[r], into.at[r], send.at[r], recv.at[r], (to_chip(7 - r) * 2 + c, t))

    def reduce_start(chunk, out, into, keep, land, ps, pr_, ss, sr):
        def produce(r):
            q = to_chip(7 - r)
            out[r] = chunk(2 * q + other).astype(BF)
            pair_copy(out, into, ps, pr_, r).start()
            keep[r] = chunk(2 * q + c).astype(BF)

        def finish(r):
            pair_copy(out, into, ps, pr_, r).wait_recv()
            keep[r] = (keep[r].astype(F32) + into[r].astype(F32)).astype(BF)

        def body(r):
            produce(r)
            finish(r - 1)
            chip_copy(keep, land, ss, sr, r - 1).start()

        produce(0)
        loop(1, 8, body)
        finish(7)

    def reduce_end(out, into, keep, land, ps, pr_, ss, sr):
        def body(r):
            chip_copy(keep, land, ss, sr, r).wait_recv()
            chip_copy(keep, land, ss, sr, r).wait_send()

        loop(0, 7, body)
        loop(0, 8, lambda r: pair_copy(out, into, ps, pr_, r).wait_send())

    loop(1, NT, lambda k: send_c(k).wait_recv())
    weights[0].wait()
    down = (pd_out, pd_in, od, rd, pd_s, pd_r, rd_s, rd_r)
    reduce_start(lambda p: dot_nt(wd[rows(p, CH), :], cs[...]), *down)

    loop(1, NT, lambda k: send_x(k).wait_recv())
    loop(1, NT, lambda k: send_tt(k).wait_recv())

    def norm_rows(block, size):
        here = rows(block, size)
        average = st[here, 0:1] * (1.0 / D)
        spread = st[here, 64:65] * (1.0 / D) - average * average
        inverse = lax.rsqrt(spread + 1e-05)
        return (xs[here, :].astype(F32) - average) * inverse, inverse

    def norm_body(block):
        here = rows(block, ROWS)
        normed, _ = norm_rows(block, ROWS)
        ain[here, :] = (normed * ag[...] + ab[...]).astype(BF)
        min_[here, :] = (normed * mg[...] + mb[...]).astype(BF)

    loop(0, NT, norm_body)

    weights[2].wait()

    def part_body(i):
        og = dot_nt(wo[rows(i, 256), :], cs[...]).astype(BF)
        pa[pl.ds(i * 2, 2), :, 0:64, :] = og.reshape(2, 2, 64, TOK)
        qq = dot_nt(wqt[rows(i, 256), :], ain[...]).astype(BF)
        pa[pl.ds(i * 2, 2), :, 64:128, :] = qq.reshape(2, 2, 64, TOK)

    loop(0, 4, part_body)
    pkv[...] = dot_nt(wqt[1024:1152, :], ain[...]).astype(BF).reshape(2, 64, TOK)
    give_a = remote(pa.at[:, other], pa_in, a_sem.at[0], a_sem.at[1], partner)
    give_kv = remote(pkv.at[other], pkv_in, a_sem.at[2], a_sem.at[3], partner)
    give_a.start()
    give_kv.start()
    give_a.wait_recv()
    give_kv.wait_recv()
    kv_pair = (pkv[c].astype(F32) + pkv_in[...].astype(F32)).astype(BF)

    def send_a(s):
        return remote(sa.at[to_chip(s)], ra.at[s], sa_s.at[s], sa_r.at[s], (to_chip(s) * 2 + c, t))

    def sum_a(s):
        q = to_chip(s)
        sa[q, 0:128, :] = (pa[q, c].astype(F32) + pa_in[q].astype(F32)).astype(BF)
        sa[q, 128:192, :] = kv_pair

    def start_a(i):
        sum_a(8 - i)
        send_a(8 - i).start()

    loop(1, 8, start_a)
    sum_a(0)

    weights[3].wait()
    up = (ph_out, ph_in, oh, rh, ph_s, ph_r, rh_s, rh_r)
    reduce_start(lambda p: dot_nn(min_[...], wu[:, rows(p, CH)]), *up)
    ain_t[...] = ain[...].T
    min_t[...] = min_[...].T

    loop(1, 8, lambda s: send_a(s).wait_recv())
    parts = []
    for i in range(3):
        acc = sa[mine, i * 64 : (i + 1) * 64, :].astype(F32)
        for s in range(1, 8):
            acc = acc + ra[s, i * 64 : (i + 1) * 64, :].astype(F32)
        parts.append(acc)
    og = parts[0].astype(BF)
    co, si = cosine[...], sine[...]
    queries_f = rotate(parts[1], co, si)
    queries = queries_f.astype(BF)
    kvx[c] = jnp.where(c == 0, rotate(parts[2], co, si), parts[2]).astype(BF)
    give = remote(kvx.at[c], kvx.at[c], kv_sem.at[0], kv_sem.at[1], partner)
    give.start()
    queries_t = queries_f.T.astype(BF)
    og_tf = og.astype(F32).T
    og_t = og_tf.astype(BF)
    give.wait_recv()
    keys = kvx[0]
    values = kvx[1]
    scaling = 1.0 / math.sqrt(HD)
    key_grad = jnp.zeros((HD, TOK), F32)
    value_grad = jnp.zeros((HD, TOK), F32)
    outs, qgs = [], []
    for n in range(4):
        low, high = n * 128, (n + 1) * 128
        scores = dot_nn(queries_t[low:high], keys) * scaling
        causal = lax.broadcasted_iota(jnp.int32, (128, TOK), 0) + low >= lax.broadcasted_iota(
            jnp.int32, (128, TOK), 1
        )
        raised = jnp.where(causal, jnp.exp(scores), 0.0)
        prob = raised / jnp.sum(raised, -1, keepdims=True)
        prob_low = prob.astype(BF)
        head = dot_nt(prob_low, values).astype(BF).astype(F32)
        dropped = dot_nn(og_t[low:high], values)
        row_dot = jnp.sum(og_tf[low:high] * head, -1, keepdims=True)
        score_grad = (prob * (dropped - row_dot) * scaling).astype(BF)
        qgs.append(dot_nt(keys, score_grad))
        key_grad = key_grad + dot_nn(queries[:, low:high], score_grad)
        value_grad = value_grad + dot_nn(og[:, low:high], prob_low)
        outs.append(head.T)
    hq[d, 0:64, :] = jnp.concatenate(outs, 1).astype(BF)
    hq[d, 64:128, :] = unrotate(jnp.concatenate(qgs, 1), co, si).astype(BF)
    pp[0] = unrotate(key_grad, co, si).astype(BF)
    pp[1] = value_grad.astype(BF)

    def send_hq(s):
        return remote(hq.at[d], hq.at[d], hq_s.at[s], hq_r.at[s], (to_chip(s) * 2 + c, t))

    def wait_hq(s):
        p = from_chip(s) * 2 + c
        remote(hq.at[p], hq.at[p], hq_s.at[s], hq_r.at[s], (to_chip(s) * 2 + c, t)).wait_recv()

    def pass_hq(s, core):
        p = from_chip(s) * 2 + core
        return remote(hq.at[p], hq.at[p], fh_s.at[s], fh_r.at[s], partner)

    give_pp = remote(pp.at[other], pp_in, pp_sem.at[0], pp_sem.at[1], partner)
    give_pp.start()
    loop(1, 8, lambda i: send_hq(8 - i).start())
    pass_hq(0, c).start()
    give_pp.wait_recv()
    psum[...] = (pp[c].astype(F32) + pp_in[...].astype(F32)).astype(BF)

    def send_pr(s):
        return remote(psum, pr.at[s], pr_s.at[s], pr_r.at[s], (to_chip(s) * 2 + c, t))

    loop(1, 8, lambda i: send_pr(8 - i).start())

    reduce_end(*down)
    reduce_end(*up)
    for h in range(2):
        cols = slice(h * 128, (h + 1) * 128)
        hid = oh[7, :, cols].astype(F32)
        for r in range(7):
            hid = hid + rh[r, :, cols].astype(F32)
        hid = hid.T
        dact = od[7, cols, :].astype(F32)
        for r in range(7):
            dact = dact + rd[r, cols, :].astype(F32)
        value, slope = gelu_parts(hid)
        ah[d, h * 128 : (h + 1) * 128, :] = value.astype(BF)
        ah[d, CH + h * 128 : CH + (h + 1) * 128, :] = (dact * slope).astype(BF)

    def send_ah(s):
        return remote(ah.at[d], ah.at[d], ah_s.at[s], ah_r.at[s], (to_chip(s) * 2 + c, t))

    def wait_ah(s):
        p = from_chip(s) * 2 + c
        remote(ah.at[p], ah.at[p], ah_s.at[s], ah_r.at[s], (to_chip(s) * 2 + c, t)).wait_recv()

    def pass_ah(s, core):
        p = from_chip(s) * 2 + core
        return remote(ah.at[p], ah.at[p], fa_s.at[s], fa_r.at[s], partner)

    loop(1, 8, lambda s: send_ah(s).start())
    pass_ah(0, c).start()

    def hq_body(s):
        wait_hq(s)
        pass_hq(s, c).start()

    loop(1, 8, hq_body)
    loop(1, 8, lambda s: send_pr(s).wait_recv())
    acc = psum[...].astype(F32)
    for s in range(1, 8):
        acc = acc + pr[s].astype(F32)
    there = rows(16 + c, 64)
    proj[there, :] = acc.astype(BF)
    give_pj = remote(proj.at[there], proj.at[there], pj_sem.at[0], pj_sem.at[1], partner)
    give_pj.start()
    loop(0, 8, lambda s: pass_hq(s, other).wait_recv())
    give_pj.wait_recv()

    def go_body(i):
        heads = hq[pl.ds(i * 4, 4), 0:64, :].reshape(256, TOK)
        wo[rows(i, 256), :] = dot_nn(heads, cs[...]).astype(BF)
        proj[rows(i, 256), :] = hq[pl.ds(i * 4, 4), 64:128, :].reshape(256, TOK)

    loop(0, 4, go_body)
    out_o_copy = pltpu.make_async_copy(wo, out_o, o_sem.at[0])
    out_o_copy.start()

    def ab_body(i):
        abt[rows(i, 128), :] = dot_nn(wq[rows(i, 128), :], proj[...])
        wq[rows(i, 128), :] = dot_nt(ain_t[rows(i, 128), :], proj[...]).astype(BF)

    loop(0, 4, ab_body)
    out_q_copy = pltpu.make_async_copy(wq, out_q, o_sem.at[1])
    out_q_copy.start()

    mbt[...] = jnp.zeros((W, TOK), F32)

    def out_d_copy(p):
        return pltpu.make_async_copy(wd.at[rows(p, CH)], out_d.at[rows(p, CH)], d_sem.at[p])

    def out_u_copy(p):
        return pltpu.make_async_copy(wu.at[:, rows(p, CH)], out_u.at[:, rows(p, CH)], u_sem.at[p])

    def consume(p):
        wd[rows(p, CH), :] = dot_nn(ah[p, 0:CH, :], cs[...]).astype(BF)
        out_d_copy(p).start()
        mbt[...] += dot_nn(wu[:, rows(p, CH)], ah[p, CH : 2 * CH, :])
        wu[:, rows(p, CH)] = dot_nt(min_t[...], ah[p, CH : 2 * CH, :]).astype(BF)
        out_u_copy(p).start()

    consume(d)
    pass_ah(0, other).wait_recv()
    consume(d + 1 - 2 * c)

    def ff_body(s):
        wait_ah(s)
        pass_ah(s, c).start()
        consume(from_chip(s) * 2 + c)
        pass_ah(s, other).wait_recv()
        consume(from_chip(s) * 2 + other)

    loop(1, 8, ff_body)

    lane2 = lax.broadcasted_iota(jnp.int32, (128, 128), 1)

    def tail_body(n):
        here = rows(n, 128)
        a_back = abt[:, here].T
        m_back = mbt[:, here].T
        normed, _ = norm_rows(n, 128)
        grad = a_back * ag[...] + m_back * mg[...]
        ngb[here, :] = grad.astype(BF)
        mom[here, :] = jnp.where(
            lane2 < 64, jnp.sum(grad, 1, keepdims=True), jnp.sum(grad * normed, 1, keepdims=True)
        )
        sums = jnp.concatenate(
            [
                jnp.sum(a_back * normed, 0, keepdims=True),
                jnp.sum(a_back, 0, keepdims=True),
                jnp.sum(m_back * normed, 0, keepdims=True),
                jnp.sum(m_back, 0, keepdims=True),
                jnp.zeros((4, W), F32),
            ],
            0,
        )
        nrm[...] += sums

    nrm[...] = jnp.zeros((8, W), F32)
    loop(0, 4, tail_body)

    def send_ng(k):
        p = (t + k) % NT
        return remote(ngb.at[rows(p, ROWS)], ngr.at[k], ng_s.at[k], ng_r.at[k], (d, p))

    def send_mo(k):
        p = (t + k) % NT
        return remote(mom.at[rows(p, ROWS)], momr.at[k], mo_s.at[k], mo_r.at[k], (d, p))

    def send_nr(k):
        return remote(nrm, nrmr.at[k], nr_s.at[k], nr_r.at[k], (d, (t + k) % NT))

    def start_tail(k):
        send_mo(k).start()
        send_ng(k).start()
        send_nr(k).start()

    loop(1, NT, start_tail)
    loop(1, NT, lambda k: send_mo(k).wait_recv())
    acc = mom[own, :]
    for k in range(1, NT):
        acc = acc + momr[k]
    m2[0] = acc

    def send_m2(k):
        return remote(m2.at[0], m2.at[k], m2_s.at[k], m2_r.at[k], ((d + k) % ND, t))

    loop(1, ND, lambda k: send_m2(k).start())
    loop(1, NT, lambda k: send_ng(k).wait_recv())
    loop(1, NT, lambda k: send_nr(k).wait_recv())
    norm_total = nrm[...]
    for k in range(1, NT):
        norm_total = norm_total + nrmr[k]
    out_n[...] = norm_total[0:4, :]
    grad = ngb[own, :].astype(F32)
    for k in range(1, NT):
        grad = grad + ngr[k].astype(F32)
    loop(1, ND, lambda k: send_m2(k).wait_recv())
    moments = m2[0]
    for k in range(1, ND):
        moments = moments + m2[k]
    first = moments[:, 0:1] * (1.0 / D)
    second = moments[:, 64:65] * (1.0 / D)
    normed, inverse = norm_rows(t, ROWS)
    out_x[...] = (c_loc[...].astype(F32) + inverse * (grad - first - normed * second)).astype(BF)

    def drain_t(k):
        send_c(k).wait_send()
        send_x(k).wait_send()
        send_tt(k).wait_send()
        send_mo(k).wait_send()
        send_ng(k).wait_send()
        send_nr(k).wait_send()

    def drain_d(k):
        send_st(k).wait_send()
        send_m2(k).wait_send()

    def drain_s(s):
        send_a(s).wait_send()
        send_hq(s).wait_send()
        send_pr(s).wait_send()
        send_ah(s).wait_send()

    def drain_p(s):
        pass_hq(s, c).wait_send()
        pass_ah(s, c).wait_send()

    def drain_o(p):
        out_d_copy(p).wait()
        out_u_copy(p).wait()

    loop(1, NT, drain_t)
    loop(1, ND, drain_d)
    loop(1, 8, drain_s)
    loop(0, 8, drain_p)
    give_a.wait_send()
    give_kv.wait_send()
    give.wait_send()
    give_pp.wait_send()
    give_pj.wait_send()
    out_o_copy.wait()
    out_q_copy.wait()
    loop(0, ND, drain_o)


def on_device(
    block_input, cotangent, attn_gain, attn_bias, mlp_gain, mlp_bias, w_qkv, w_out, w_up, w_down
):
    cosine, sine = rope_columns()
    vmem = pl.BlockSpec(memory_space=pltpu.VMEM)
    hbm = pl.BlockSpec(memory_space=pl.ANY)
    dma = pltpu.SemaphoreType.DMA

    def buf(*shape):
        return pltpu.VMEM(shape, BF)

    def wide(*shape):
        return pltpu.VMEM(shape, F32)

    buffers = [
        buf(TOK, W), buf(TOK, W), wide(ND, ROWS, 128), wide(TOK, 128),
        buf(W, QKV), buf(QKV, W), buf(1024, W), buf(W, FF), buf(FF, W),
        buf(TOK, W), buf(TOK, W), buf(W, TOK), buf(W, TOK),
        buf(8, 2, 128, TOK), buf(2, 64, TOK), buf(8, 128, TOK), buf(64, TOK),
        buf(8, 192, TOK), buf(8, 192, TOK), buf(2, 64, TOK),
        buf(8, CH, TOK), buf(8, CH, TOK), buf(8, CH, TOK), buf(7, CH, TOK),
        buf(8, TOK, CH), buf(8, TOK, CH), buf(8, TOK, CH), buf(7, TOK, CH),
        buf(ND, 2 * CH, TOK), buf(ND, 128, TOK), buf(QKV, TOK),
        buf(2, 64, TOK), buf(64, TOK), buf(64, TOK), buf(8, 64, TOK),
        wide(W, TOK), wide(W, TOK), buf(TOK, W), buf(NT, ROWS, W),
        wide(TOK, 128), wide(NT, ROWS, 128), wide(8, W), wide(NT, 8, W), wide(ND, ROWS, 128),
    ]
    semaphores = [dma((n,)) for n in (4, 8, 8, 8, 8, 16, 16, 8, 8)]
    semaphores += [dma((n,)) for n in (4, 8, 8, 2)]
    semaphores += [dma((8,))] * 8
    semaphores += [dma((n,)) for n in (8, 8, 8, 8, 8, 8, 8, 8, 2, 8, 8, 2)]
    semaphores += [dma((n,)) for n in (2, 16, 16, 8, 8, 8, 8, 8, 8, 16, 16)]
    return pl.pallas_call(
        kernel,
        out_shape=(
            jax.ShapeDtypeStruct((ROWS, W), BF),
            jax.ShapeDtypeStruct((4, W), F32),
            jax.ShapeDtypeStruct((W, QKV), BF),
            jax.ShapeDtypeStruct((1024, W), BF),
            jax.ShapeDtypeStruct((W, FF), BF),
            jax.ShapeDtypeStruct((FF, W), BF),
        ),
        in_specs=[vmem] * 8 + [hbm] * 4,
        out_specs=(vmem, vmem, hbm, hbm, hbm, hbm),
        scratch_shapes=buffers + semaphores,
        compiler_params=pltpu.CompilerParams(
            collective_id=0, has_side_effects=True, vmem_limit_bytes=60 * 2**20
        ),
        cost_estimate=pl.CostEstimate(flops=14 * 10**9, bytes_accessed=21 * 10**6, transcendentals=10**6),
        name="block_backward",
    )(
        block_input, cotangent, attn_gain[None], attn_bias[None], mlp_gain[None], mlp_bias[None],
        cosine, sine, w_qkv, w_out, w_up, w_down,
    )


def solution(mesh):
    return jax.shard_map(
        on_device,
        mesh=mesh,
        in_specs=(
            P("tensor", "dp"),
            P("tensor", "dp"),
            P("dp"),
            P("dp"),
            P("dp"),
            P("dp"),
            P("dp", "tensor"),
            P("tensor", "dp"),
            P("dp", "tensor"),
            P("tensor", "dp"),
        ),
        out_specs=(
            P("tensor", "dp"),
            P(None, "dp"),
            P("dp", "tensor"),
            P("tensor", "dp"),
            P("dp", "tensor"),
            P("tensor", "dp"),
        ),
        check_vma=False,
    )
```

time: 882 us -> 245 us (0.28)
  waiting for transfers between devices: 625 us -> 0 us
  Pallas kernels: 0 us -> 226 us
  blocking collectives: 168 us -> 0 us
  matrix products: 50.6 us -> 0 us
  between operations: 14.1 us -> 0.67 us
  other arithmetic: 12.9 us -> 1.05 us
    reduce_scatter x5 -> x0, waiting for transfers between devices: 326 us -> none  [the longest x1 73.8 us: on_device(): lax.psum_scatter(back_part.astype(jnp.bfloat16), 'tensor', scatter_dimens...]
    pallas_call x0 -> x1, Pallas kernels: none -> 226 us  [on_device(): pl.pallas_call(kernel, out_shape=(jax.ShapeDtypeStruct((ROWS, W), BF), ja...]
    psum x2 -> x0, waiting for transfers between devices: 174 us -> none  [the longest x1 115 us: on_device(): lax.psum(pair_part.astype(jnp.bfloat16), 'dp').astype(jnp.float32)]
    all_gather x4 -> x0, waiting for transfers between devices: 124 us -> none  [the longest x1 36.9 us: on_device(): fragment = lax.all_gather(hidden_grad, 'dp', axis=0, tiled=True)]
    all_gather x3 -> x0, blocking collectives: 88 us -> none  [the longest x1 29.6 us: on_device(): lax.all_gather(attn_local, 'tensor', axis=0, tiled=True)]
    psum x3 -> x0, blocking collectives: 79.8 us -> none  [the longest x1 32.8 us: on_device(): lax.psum((jnp.sum(normed_grad, 1), jnp.sum(normed_grad * normed, 1)), 'dp')]
    dot_general x18 -> x0, matrix products: 50.6 us -> none  [the longest x8 27.9 us: across_tokens(): lax.dot_general(weights, token_major, (((0,), (1,)), ((), ())), preferred...]
    unnamed x29 -> x10, local copies, waits for them, and re-layouts: 3.51 us -> 13.3 us
  transfers between devices with their start and end apart: 11 -> 0, of which waited for: 11 -> 0; matrix products, arithmetic and copies ran while one was open for 7% -> 0% of each run, Pallas kernels for 0% -> 0%
where the time goes in v1:
time: 245 us; the launch traced here: 241 us
  Pallas kernels  226 us (92%)
  local copies, waits for them, and re-layouts  13.3 us (5%)
    pallas_call x1, Pallas kernels, on_device(): pl.pallas_call(kernel, out_shape=(jax.ShapeDtypeStruct((ROWS, W), BF), ja...  226 us
    unnamed x10, local copies, waits for them, and re-layouts  13.3 us

profile of v1, /device:TPU:1, one launch (start us, length us, event | category | flops | bytes accessed | tf_op | source)
XLA Modules:
  0.0 240.6 jit_solution(9860106767641627902)
XLA Ops:
  0.7 0.3 multiply_sine_fusion
  1.0 0.7 pad_maximum_fusion
  1.7 225.6 %block_backward.1 = (bf16[64,512]{1,0:T(8,128)(2,1)}, f32[4,512]{1,0:T(4,128)}, bf16[512,1152]{1,0:T(8,128)(2,1)}, bf16[1024,512]{1,0:T(8,128)(2,1)}, bf16[512,4...) custom-call(bf16[64,512]{1,0:T(8,128)(2,1)} %x_loc.1, bf16[64,512]{1,0:T(8,128)(2,1)} %c_loc.1, f32[1,512]{1,0:T(1,128)} %bitcast.4, ...), custom_call_target="tpu_custom_call" | custom-call | flops 14000000000 | bytes 21000000 | tf_op jit(solution)/shard_map/block_backward/pallas_call | solution.py:564
  227.3 0.0 copy-start.1
  227.3 1.6 copy.22
  228.9 1.3 copy.23
  230.2 2.4 copy.24
  232.6 2.3 copy.25
  234.9 0.0 copy-done.1
  234.9 0.0 copy-start
  234.9 2.1 copy.26
  237.0 1.6 copy-done
  238.6 2.0 copy.27
  (2 shorter events, 0.0 us)
Async XLA Ops:
  227.3 7.6 %copy-start.1 = (bf16[512,4096]{1,0:T(8,128)(2,1)S(1)}, bf16[512,4096]{1,0:T(8,128)(2,1)}, u32[]{:S(2)}) copy-start(bf16[512,4096]{1,0:T(8,128)(2,1)} %get-tuple-element.20) | copy-start | bytes 12582916
  234.9 3.7 %copy-start = (bf16[4096,512]{1,0:T(8,128)(2,1)S(1)}, bf16[4096,512]{1,0:T(8,128)(2,1)}, u32[]{:S(2)}) copy-start(bf16[4096,512]{1,0:T(8,128)(2,1)} %get-tuple-element.21) | copy-start | bytes 12582916

commit v2 on v1

v2 whole, which is shorter than its diff:
```python
import functools
import math

import jax
import jax.numpy as jnp
from jax import lax
from jax.experimental import pallas as pl
from jax.experimental.pallas import tpu as pltpu
from jax.sharding import PartitionSpec as P

D = 8192
HD = 64
LENGTH = 512
TOK = 512
W = 512
ROWS = 64
NT = 8
ND = 16
FF = 4096
CH = 256
QKV = 1152
MESH = pl.DeviceIdType.MESH
BF = jnp.bfloat16
F32 = jnp.float32


def dot_nn(a, b):
    return jnp.dot(a, b, preferred_element_type=F32)


def dot_nt(a, b):
    return lax.dot_general(a, b, (((1,), (1,)), ((), ())), preferred_element_type=F32)


def gelu_parts(v):
    half = 0.5 * (1.0 + lax.erf(v * 0.7071067811865476))
    return v * half, half + v * jnp.exp(-0.5 * v * v) * 0.3989422804014327


def rope_columns():
    halfway = HD // 2
    position = (jnp.arange(TOK) % LENGTH).astype(F32)
    frequency = 10000.0 ** (-2.0 * jnp.arange(halfway).astype(F32) / HD)
    angle = frequency[:, None] * position[None, :]
    cosine = jnp.concatenate([jnp.cos(angle), jnp.cos(angle)], 0)
    sine = jnp.concatenate([jnp.sin(angle), jnp.sin(angle)], 0)
    return cosine, sine


def rotate(v, cosine, sine):
    turned = jnp.concatenate([-v[32:], v[:32]], 0)
    return v * cosine + turned * sine


def unrotate(v, cosine, sine):
    scaled = v * sine
    back = jnp.concatenate([scaled[32:], -scaled[:32]], 0)
    return v * cosine + back


class Reduce:
    def __init__(self, place, part, zin, in1, in2m, in2p, zfin, send, recv, split):
        self.place, self.part, self.zin, self.in1 = place, part, zin, in1
        self.in2m, self.in2p, self.zfin, self.send, self.recv = in2m, in2p, zfin, send, recv
        size, a, ma, mb = split
        self.a, self.size = a, size
        self.jobs = ((0, 0, ma, a), (1, 0, ma, a), (0, a, mb, size))

    def copy(self, src, dst, k, device):
        return self.place.remote(src, dst, self.send.at[k], self.recv.at[k], device)

    def block(self, plane, j):
        return self.part.at[self.place.chip(plane, j)]

    def z_first(self, j):
        src = self.block(1, j).at[self.a : self.size]
        return self.copy(src, self.zin.at[j], j, self.place.z_side)

    def one(self, job, way):
        plane, low, mid, high = self.jobs[job]
        here = slice(low, mid) if way == 0 else slice(mid, high)
        device = (self.place.x_up, self.place.x_down)[way]
        return self.copy(self.block(plane, 2).at[here], self.in1.at[plane, here], 4 + 2 * job + way, device)

    def two(self, job, way):
        plane, low, _, high = self.jobs[job]
        here = slice(low, high)
        device = (self.place.x_up, self.place.x_down)[way]
        land = (self.in2m, self.in2p)[way]
        return self.copy(self.block(plane, (1, 3)[way]).at[here], land.at[plane, here], 10 + 2 * job + way, device)

    def z_last(self):
        return self.copy(self.block(1, 0).at[0 : self.a], self.zfin, 16, self.place.z_side)

    def add(self, plane, j, here, more):
        target = self.block(plane, j)
        total = target[here].astype(F32)
        for term in more:
            total = total + term.astype(F32)
        target[here] = total.astype(BF)

    def start(self):
        for job in (1, 0):
            for way in (0, 1):
                self.one(job, way).start()

    def z_merge(self):
        for j in (2, 1, 0, 3):
            self.z_first(j).wait_recv()
            self.add(0, j, slice(self.a, self.size), [self.zin[j]])
            if j == 2:
                self.one(2, 0).start()
                self.one(2, 1).start()

    def step_two(self, job):
        plane, low, mid, high = self.jobs[job]
        for way, here in ((0, slice(low, mid)), (1, slice(mid, high))):
            self.one(job, way).wait_recv()
            self.add(plane, (1, 3)[way], here, [self.in1[plane, here]])
            self.two(job, way).start()

    def step_z(self):
        self.two(1, 0).wait_recv()
        self.two(1, 1).wait_recv()
        here = slice(0, self.a)
        self.add(1, 0, here, [self.in2m[1, here], self.in2p[1, here]])
        self.z_last().start()

    def finish(self):
        for job in (0, 2):
            self.two(job, 0).wait_recv()
            self.two(job, 1).wait_recv()
        self.z_last().wait_recv()

    def total(self, low, high, cols=slice(None)):
        out = self.block(0, 0)[low:high, cols].astype(F32)
        out = out + self.in2m[0, low:high, cols].astype(F32) + self.in2p[0, low:high, cols].astype(F32)
        top = min(high, self.a)
        if top <= low:
            return out
        upper = out[: top - low] + self.zfin[low:top, cols].astype(F32)
        return upper if top == high else jnp.concatenate([upper, out[top - low :]], 0)

    def drain(self):
        for j in range(4):
            self.z_first(j).wait_send()
        for job in range(3):
            for way in range(2):
                self.one(job, way).wait_send()
                self.two(job, way).wait_send()
        self.z_last().wait_send()


class Gather:
    def __init__(self, place, buf, send, recv, split):
        self.place, self.buf, self.send, self.recv = place, buf, send, recv
        size, a, mo, ma = split
        up, down, side = place.x_up, place.x_down, place.z_side
        own, left, right, far = (0, 0), (0, 3), (0, 1), (0, 2)
        z_own, z_left, z_right, z_far = (1, 0), (1, 3), (1, 1), (1, 2)
        self.moves = (
            (own, left, 0, size, up),
            (own, right, 0, size, down),
            (own, z_own, 0, size, side),
            (left, far, 0, mo, up),
            (right, far, mo, size, down),
            (left, z_left, a, size, side),
            (right, z_right, a, size, side),
            (far, z_far, a, size, side),
            (z_own, z_left, 0, a, up),
            (z_own, z_right, 0, a, down),
            (z_left, z_far, 0, ma, up),
            (z_right, z_far, ma, a, down),
        )

    def index(self, where):
        return self.place.chip(*where) * 2 + self.place.c

    def copy(self, index, low, high, k, device):
        at = self.buf.at[index, low:high]
        return self.place.remote(at, at, self.send.at[k], self.recv.at[k], device)

    def go(self, *moves):
        for k in moves:
            src, _, low, high, device = self.moves[k]
            self.copy(self.index(src), low, high, k, device).start()

    def wait(self, *moves):
        for k in moves:
            _, dst, low, high, device = self.moves[k]
            self.copy(self.index(dst), low, high, k, device).wait_recv()

    def hand(self, plane, j, core):
        index = self.place.chip(plane, j) * 2 + core
        k = 12 + j + 4 * plane
        at = self.buf.at[index]
        return self.place.remote(at, at, self.send.at[k], self.recv.at[k], self.place.partner)

    def give(self, *wheres):
        for plane, j in wheres:
            self.hand(plane, j, self.place.c).start()

    def take(self, plane, j):
        self.hand(plane, j, self.place.other).wait_recv()

    def start(self):
        self.go(0, 1, 2)
        self.give((0, 0))

    def step_one(self):
        self.wait(0)
        self.go(3, 5)
        self.wait(1)
        self.go(4, 6)
        self.wait(2)
        self.go(8, 9)
        self.give((0, 3), (0, 1), (1, 0))

    def step_two(self):
        self.wait(3, 4)
        self.go(7)
        self.wait(8)
        self.go(10)
        self.wait(9)
        self.go(11)
        self.give((0, 2))

    def step_three(self):
        self.wait(5, 6)
        self.give((1, 3), (1, 1))
        self.wait(7, 10, 11)
        self.give((1, 2))

    def drain(self):
        for k, (src, _, low, high, device) in enumerate(self.moves):
            self.copy(self.index(src), low, high, k, device).wait_send()
        for plane in range(2):
            for j in range(4):
                self.hand(plane, j, self.place.c).wait_send()


class Place:
    def __init__(self):
        self.d = d = lax.axis_index("dp")
        self.t = t = lax.axis_index("tensor")
        self.c = d % 2
        self.other = 1 - self.c
        self.x = x = (d // 2) % 4
        self.z = z = d // 8
        self.partner = (d + 1 - 2 * self.c, t)
        self.x_up = (z * 8 + ((x + 1) % 4) * 2 + self.c, t)
        self.x_down = (z * 8 + ((x + 3) % 4) * 2 + self.c, t)
        self.z_side = ((1 - z) * 8 + x * 2 + self.c, t)
        self.x_even = (z * 8 + (x + 1 - 2 * (x % 2)) * 2 + self.c, t)
        self.x_odd = (z * 8 + ((x + 3 + 2 * (x % 2)) % 4) * 2 + self.c, t)

    def chip(self, plane, j):
        return ((self.z + plane) % 2) * 4 + (self.x + j) % 4

    def remote(self, src, dst, send, recv, device):
        return pltpu.make_async_remote_copy(
            src_ref=src, dst_ref=dst, send_sem=send, recv_sem=recv, device_id=device, device_id_type=MESH
        )


class Doubling:
    def __init__(self, place, out, into, send, recv):
        self.place, self.out, self.into, self.send, self.recv = place, out, into, send, recv
        self.devices = (place.z_side, place.x_even, place.x_odd)

    def copy(self, k):
        return self.place.remote(
            self.out.at[k], self.into.at[k], self.send.at[k], self.recv.at[k], self.devices[k]
        )

    def start(self, value):
        self.out[0] = value
        self.copy(0).start()

    def step(self, k):
        self.copy(k - 1).wait_recv()
        total = self.out[k - 1].astype(F32) + self.into[k - 1].astype(F32)
        if k == 3:
            return total
        self.out[k] = total.astype(BF)
        self.copy(k).start()
        return total

    def drain(self):
        for k in range(3):
            self.copy(k).wait_send()


def kernel(
    x_loc, c_loc, ag, ab, mg, mb, cosine, sine, wq_hbm, wo_hbm, wu_hbm, wd_hbm,
    out_x, out_n, out_q, out_o, out_u, out_d,
    xs, cs, st_in, st, wq, wqt, wo, wu, wd, ain, min_, ain_t, min_t,
    pa, pa_in, pkv, pkv_in, kvo, kvi, kvx,
    t_part, t_z, t_1, t_2m, t_2p, t_f,
    d_out, d_in, d_part, d_z, d_1, d_2m, d_2p, d_f,
    h_out, h_in, h_part, h_z, h_1, h_2m, h_2p, h_f,
    act, hid, hq, proj, pp, pp_in, ppo, ppi,
    abt, mbt, ngb, ngr, mom, momr, nrm, nrmr, m2,
    w_sem, x_s, x_r, c_s, c_r, st_s, st_r, tt_s, tt_r,
    p_s, p_r, dp_s, dp_r, hp_s, hp_r, ts, tr, ds, dr, hs, hr, kv_s, kv_r, pp_s, pp_r,
    as_, ar, gs, gr, qs, qr, o_sem, u_sem, d_sem,
    ng_s, ng_r, mo_s, mo_r, nr_s, nr_r, m2_s, m2_r,
):
    place = Place()
    d, t, c, other, partner, remote = place.d, place.t, place.c, place.other, place.partner, place.remote

    def rows(index, size):
        return pl.ds(pl.multiple_of(index * size, size), size)

    def loop(low, high, f):
        def body(k, carry):
            f(k)
            return carry

        lax.fori_loop(low, high, body, 0)

    weights = [
        pltpu.make_async_copy(src, dst, w_sem.at[i])
        for i, (src, dst) in enumerate([(wd_hbm, wd), (wq_hbm, wq), (wo_hbm, wo), (wu_hbm, wu)])
    ]
    for copy in weights:
        copy.start()

    barrier = pltpu.get_barrier_semaphore()
    loop(
        1, NT,
        lambda k: pl.semaphore_signal(barrier, inc=1, device_id=(d, (t + k) % NT), device_id_type=MESH),
    )
    loop(
        1, ND,
        lambda k: pl.semaphore_signal(barrier, inc=1, device_id=((d + k) % ND, t), device_id_type=MESH),
    )
    pl.semaphore_wait(barrier, NT - 1 + ND - 1)

    own = rows(t, ROWS)

    def send_c(k):
        return remote(c_loc, cs.at[own], c_s.at[k], c_r.at[k], (d, (t + k) % NT))

    def send_x(k):
        return remote(x_loc, xs.at[own], x_s.at[k], x_r.at[k], (d, (t + k) % NT))

    def send_st(k):
        return remote(st_in.at[0], st_in.at[k], st_s.at[k], st_r.at[k], ((d + k) % ND, t))

    def send_tt(k):
        return remote(st.at[own], st.at[own], tt_s.at[k], tt_r.at[k], (d, (t + k) % NT))

    loop(1, NT, lambda k: send_c(k).start())
    lane = lax.broadcasted_iota(jnp.int32, (ROWS, 128), 1)
    xf = x_loc[...].astype(F32)
    st_in[0] = jnp.where(
        lane < 64, jnp.sum(xf, 1, keepdims=True), jnp.sum(xf * xf, 1, keepdims=True)
    )
    loop(1, ND, lambda k: send_st(k).start())
    cs[own, :] = c_loc[...]
    xs[own, :] = x_loc[...]
    weights[1].wait()
    for i in range(QKV // 128):
        wqt[i * 128 : (i + 1) * 128, :] = wq[:, i * 128 : (i + 1) * 128].T
    loop(1, ND, lambda k: send_st(k).wait_recv())
    total = st_in[0]
    for k in range(1, ND):
        total = total + st_in[k]
    st[own, :] = total
    loop(1, NT, lambda k: send_tt(k).start())
    loop(1, NT, lambda k: send_c(k).wait_recv())
    loop(1, NT, lambda k: send_x(k).start())

    def produce(chunk, job, out, into, send, recv):
        def pair(q, k):
            return remote(out.at[q], into.at[q], send.at[k], recv.at[k], partner)

        def body(i):
            @pl.when(i < 4)
            def _():
                j = (2 + 3 * i) % 4
                for plane in (1, 0):
                    q = place.chip(plane, j)
                    out[q] = chunk(2 * q + other).astype(BF)
                    pair(q, 2 * i + plane).start()
                for plane in (1, 0):
                    q = place.chip(plane, j)
                    job.part[q] = chunk(2 * q + c).astype(BF)

            @pl.when(i > 0)
            def _():
                j = (3 * i - 1) % 4
                for plane in (1, 0):
                    q = place.chip(plane, j)
                    pair(q, 2 * (i - 1) + plane).wait_recv()
                    job.part[q] = (job.part[q].astype(F32) + into[q].astype(F32)).astype(BF)
                    if plane == 1:
                        job.z_first(j).start()

            @pl.when(i == 1)
            def _():
                job.start()

        loop(0, 5, body)

    def pair_drain(out, into, send, recv):
        loop(0, 8, lambda k: remote(out.at[k], into.at[k], send.at[k], recv.at[k], partner).wait_send())

    down = Reduce(place, d_part, d_z, d_1, d_2m, d_2p, d_f, ds, dr, (256, 144, 80, 192))
    up = Reduce(place, h_part, h_z, h_1, h_2m, h_2p, h_f, hs, hr, (512, 288, 160, 384))
    attn = Reduce(place, t_part, t_z, t_1, t_2m, t_2p, t_f, ts, tr, (128, 80, 48, 96))
    weights[0].wait()
    produce(lambda p: dot_nt(wd[rows(p, CH), :], cs[...]), down, d_out, d_in, dp_s, dp_r)

    loop(1, NT, lambda k: send_x(k).wait_recv())
    loop(1, NT, lambda k: send_tt(k).wait_recv())

    def norm_rows(block, size):
        here = rows(block, size)
        average = st[here, 0:1] * (1.0 / D)
        spread = st[here, 64:65] * (1.0 / D) - average * average
        inverse = lax.rsqrt(spread + 1e-05)
        return (xs[here, :].astype(F32) - average) * inverse, inverse

    def norm_body(block):
        here = rows(block, ROWS)
        normed, _ = norm_rows(block, ROWS)
        ain[here, :] = (normed * ag[...] + ab[...]).astype(BF)
        min_[here, :] = (normed * mg[...] + mb[...]).astype(BF)

    loop(0, NT, norm_body)

    weights[2].wait()

    def part_body(i):
        og = dot_nt(wo[rows(i, 256), :], cs[...]).astype(BF)
        pa[pl.ds(i * 2, 2), :, 0:64, :] = og.reshape(2, 2, 64, TOK)
        qq = dot_nt(wqt[rows(i, 256), :], ain[...]).astype(BF)
        pa[pl.ds(i * 2, 2), :, 64:128, :] = qq.reshape(2, 2, 64, TOK)

    pkv[...] = dot_nt(wqt[1024:1152, :], ain[...]).astype(BF).reshape(2, 64, TOK)
    give_kv = remote(pkv.at[other], pkv_in, p_s.at[0], p_r.at[0], partner)
    give_kv.start()
    loop(0, 4, part_body)
    give_a = remote(pa.at[:, other], pa_in, p_s.at[1], p_r.at[1], partner)
    give_a.start()

    down.z_merge()
    down.step_two(1)
    down.step_two(0)

    kv_sum = Doubling(place, kvo, kvi, kv_s, kv_r)
    give_kv.wait_recv()
    kv_sum.start((pkv[c].astype(F32) + pkv_in[...].astype(F32)).astype(BF))
    give_a.wait_recv()

    def sum_a(q):
        t_part[q] = (pa[q, c].astype(F32) + pa_in[q].astype(F32)).astype(BF)

    loop(0, 8, sum_a)
    for j in (2, 1, 0, 3):
        attn.z_first(j).start()
    attn.start()

    weights[3].wait()
    produce(lambda p: dot_nn(min_[...], wu[:, rows(p, CH)]), up, h_out, h_in, hp_s, hp_r)

    down.step_two(2)
    down.step_z()
    kv_sum.step(1)
    attn.z_merge()
    attn.step_two(1)
    attn.step_two(0)
    kv_sum.step(2)
    up.z_merge()
    up.step_two(1)
    up.step_two(0)
    attn.step_two(2)
    attn.step_z()
    ain_t[...] = ain[...].T
    min_t[...] = min_[...].T

    attn.finish()
    og = attn.total(0, 64).astype(BF)
    q_sum = attn.total(64, 128)
    kv_total = kv_sum.step(3)

    co, si = cosine[...], sine[...]
    queries_f = rotate(q_sum, co, si)
    queries = queries_f.astype(BF)
    kvx[c] = jnp.where(c == 0, rotate(kv_total, co, si), kv_total).astype(BF)
    give = remote(kvx.at[c], kvx.at[c], p_s.at[2], p_r.at[2], partner)
    give.start()
    queries_t = queries_f.T.astype(BF)
    og_tf = og.astype(F32).T
    og_t = og_tf.astype(BF)
    give.wait_recv()
    keys = kvx[0]
    values = kvx[1]
    scaling = 1.0 / math.sqrt(HD)
    key_grad = jnp.zeros((HD, TOK), F32)
    value_grad = jnp.zeros((HD, TOK), F32)
    outs, qgs = [], []
    for n in range(4):
        low, high = n * 128, (n + 1) * 128
        scores = dot_nn(queries_t[low:high], keys) * scaling
        causal = lax.broadcasted_iota(jnp.int32, (128, TOK), 0) + low >= lax.broadcasted_iota(
            jnp.int32, (128, TOK), 1
        )
        raised = jnp.where(causal, jnp.exp(scores), 0.0)
        prob = raised / jnp.sum(raised, -1, keepdims=True)
        prob_low = prob.astype(BF)
        head = dot_nt(prob_low, values).astype(BF).astype(F32)
        dropped = dot_nn(og_t[low:high], values)
        row_dot = jnp.sum(og_tf[low:high] * head, -1, keepdims=True)
        score_grad = (prob * (dropped - row_dot) * scaling).astype(BF)
        qgs.append(dot_nt(keys, score_grad))
        key_grad = key_grad + dot_nn(queries[:, low:high], score_grad)
        value_grad = value_grad + dot_nn(og[:, low:high], prob_low)
        outs.append(head.T)
    hq[d, 0:64, :] = jnp.concatenate(outs, 1).astype(BF)
    hq[d, 64:128, :] = unrotate(jnp.concatenate(qgs, 1), co, si).astype(BF)
    pp[0] = unrotate(key_grad, co, si).astype(BF)
    pp[1] = value_grad.astype(BF)

    heads = Gather(place, hq, qs, qr, (128, 80, 64, 48))
    heads.start()
    give_pp = remote(pp.at[other], pp_in, p_s.at[3], p_r.at[3], partner)
    give_pp.start()

    up.step_two(2)
    up.step_z()
    give_pp.wait_recv()
    pp_sum = Doubling(place, ppo, ppi, pp_s, pp_r)
    pp_sum.start((pp[c].astype(F32) + pp_in[...].astype(F32)).astype(BF))
    heads.step_one()
    pp_sum.step(1)
    down.finish()
    up.finish()

    for h in range(2):
        cols = slice(h * 128, (h + 1) * 128)
        hidden = up.total(0, 512, cols).T
        dact = down.total(h * 128, (h + 1) * 128)
        value, slope = gelu_parts(hidden)
        act[d, cols, :] = value.astype(BF)
        hid[d, cols, :] = (dact * slope).astype(BF)

    gather_act = Gather(place, act, as_, ar, (256, 144, 128, 80))
    gather_hid = Gather(place, hid, gs, gr, (256, 144, 128, 80))
    gather_act.start()
    gather_hid.start()

    heads.step_two()
    pp_sum.step(2)
    heads.step_three()
    there = rows(16 + c, 64)
    proj[there, :] = pp_sum.step(3).astype(BF)
    give_pj = remote(proj.at[there], proj.at[there], p_s.at[4], p_r.at[4], partner)
    give_pj.start()
    for plane in range(2):
        for j in range(4):
            heads.take(plane, j)
    give_pj.wait_recv()

    def go_body(i):
        four = hq[pl.ds(i * 4, 4), 0:64, :].reshape(256, TOK)
        wo[rows(i, 256), :] = dot_nn(four, cs[...]).astype(BF)
        proj[rows(i, 256), :] = hq[pl.ds(i * 4, 4), 64:128, :].reshape(256, TOK)

    loop(0, 4, go_body)
    out_o_copy = pltpu.make_async_copy(wo, out_o, o_sem.at[0])
    out_o_copy.start()

    def ab_body(i):
        abt[rows(i, 128), :] = dot_nn(wq[rows(i, 128), :], proj[...])
        wq[rows(i, 128), :] = dot_nt(ain_t[rows(i, 128), :], proj[...]).astype(BF)

    loop(0, 4, ab_body)
    out_q_copy = pltpu.make_async_copy(wq, out_q, o_sem.at[1])
    out_q_copy.start()

    mbt[...] = jnp.zeros((W, TOK), F32)

    def out_d_copy(p):
        return pltpu.make_async_copy(wd.at[rows(p, CH)], out_d.at[rows(p, CH)], d_sem.at[p])

    def out_u_copy(p):
        return pltpu.make_async_copy(wu.at[:, rows(p, CH)], out_u.at[:, rows(p, CH)], u_sem.at[p])

    def consume(p):
        wd[rows(p, CH), :] = dot_nn(act[p], cs[...]).astype(BF)
        out_d_copy(p).start()
        mbt[...] += dot_nn(wu[:, rows(p, CH)], hid[p])
        wu[:, rows(p, CH)] = dot_nt(min_t[...], hid[p]).astype(BF)
        out_u_copy(p).start()

    def ff_body(i):
        @pl.when(i == 1)
        def _():
            gather_act.step_one()
            gather_hid.step_one()

        @pl.when(i == 3)
        def _():
            gather_act.step_two()
            gather_hid.step_two()

        @pl.when(i == 5)
        def _():
            gather_act.step_three()
            gather_hid.step_three()

        plane = i // 5 + (i + 6) // 7 - (i + 5) // 7
        k = (i + 1) % 3
        j = ((i + 1) // 3 + 1) // 2 * (1 + 2 * k - 3 * (k // 2))
        consume(place.chip(plane, j) * 2 + c)
        gather_act.take(plane, j)
        gather_hid.take(plane, j)
        consume(place.chip(plane, j) * 2 + other)

    loop(0, 8, ff_body)

    lane2 = lax.broadcasted_iota(jnp.int32, (128, 128), 1)

    def tail_body(n):
        here = rows(n, 128)
        a_back = abt[:, here].T
        m_back = mbt[:, here].T
        normed, _ = norm_rows(n, 128)
        grad = a_back * ag[...] + m_back * mg[...]
        ngb[here, :] = grad.astype(BF)
        mom[here, :] = jnp.where(
            lane2 < 64, jnp.sum(grad, 1, keepdims=True), jnp.sum(grad * normed, 1, keepdims=True)
        )
        sums = jnp.concatenate(
            [
                jnp.sum(a_back * normed, 0, keepdims=True),
                jnp.sum(a_back, 0, keepdims=True),
                jnp.sum(m_back * normed, 0, keepdims=True),
                jnp.sum(m_back, 0, keepdims=True),
                jnp.zeros((4, W), F32),
            ],
            0,
        )
        nrm[...] += sums

    nrm[...] = jnp.zeros((8, W), F32)
    loop(0, 4, tail_body)

    def send_ng(k):
        p = (t + k) % NT
        return remote(ngb.at[rows(p, ROWS)], ngr.at[k], ng_s.at[k], ng_r.at[k], (d, p))

    def send_mo(k):
        p = (t + k) % NT
        return remote(mom.at[rows(p, ROWS)], momr.at[k], mo_s.at[k], mo_r.at[k], (d, p))

    def send_nr(k):
        return remote(nrm, nrmr.at[k], nr_s.at[k], nr_r.at[k], (d, (t + k) % NT))

    def start_tail(k):
        send_mo(k).start()
        send_ng(k).start()
        send_nr(k).start()

    loop(1, NT, start_tail)
    loop(1, NT, lambda k: send_mo(k).wait_recv())
    acc = mom[own, :]
    for k in range(1, NT):
        acc = acc + momr[k]
    m2[0] = acc

    def send_m2(k):
        return remote(m2.at[0], m2.at[k], m2_s.at[k], m2_r.at[k], ((d + k) % ND, t))

    loop(1, ND, lambda k: send_m2(k).start())
    loop(1, NT, lambda k: send_ng(k).wait_recv())
    loop(1, NT, lambda k: send_nr(k).wait_recv())
    norm_total = nrm[...]
    for k in range(1, NT):
        norm_total = norm_total + nrmr[k]
    out_n[...] = norm_total[0:4, :]
    grad = ngb[own, :].astype(F32)
    for k in range(1, NT):
        grad = grad + ngr[k].astype(F32)
    loop(1, ND, lambda k: send_m2(k).wait_recv())
    moments = m2[0]
    for k in range(1, ND):
        moments = moments + m2[k]
    first = moments[:, 0:1] * (1.0 / D)
    second = moments[:, 64:65] * (1.0 / D)
    normed, inverse = norm_rows(t, ROWS)
    out_x[...] = (c_loc[...].astype(F32) + inverse * (grad - first - normed * second)).astype(BF)

    def drain_t(k):
        send_c(k).wait_send()
        send_x(k).wait_send()
        send_tt(k).wait_send()
        send_mo(k).wait_send()
        send_ng(k).wait_send()
        send_nr(k).wait_send()

    def drain_d(k):
        send_st(k).wait_send()
        send_m2(k).wait_send()

    def drain_o(p):
        out_d_copy(p).wait()
        out_u_copy(p).wait()

    loop(1, NT, drain_t)
    loop(1, ND, drain_d)
    for copy in (give_a, give_kv, give, give_pp, give_pj):
        copy.wait_send()
    pair_drain(d_out, d_in, dp_s, dp_r)
    pair_drain(h_out, h_in, hp_s, hp_r)
    for job in (down, up, attn, kv_sum, pp_sum, heads, gather_act, gather_hid):
        job.drain()
    out_o_copy.wait()
    out_q_copy.wait()
    loop(0, ND, drain_o)


def on_device(
    block_input, cotangent, attn_gain, attn_bias, mlp_gain, mlp_bias, w_qkv, w_out, w_up, w_down
):
    cosine, sine = rope_columns()
    vmem = pl.BlockSpec(memory_space=pltpu.VMEM)
    hbm = pl.BlockSpec(memory_space=pl.ANY)
    dma = pltpu.SemaphoreType.DMA

    def buf(*shape):
        return pltpu.VMEM(shape, BF)

    def wide(*shape):
        return pltpu.VMEM(shape, F32)

    def sums(size, a, width):
        return [
            buf(8, size, width), buf(4, size - a, width), buf(2, size, width),
            buf(2, size, width), buf(2, size, width), buf(a, width),
        ]

    buffers = [
        buf(TOK, W), buf(TOK, W), wide(ND, ROWS, 128), wide(TOK, 128),
        buf(W, QKV), buf(QKV, W), buf(1024, W), buf(W, FF), buf(FF, W),
        buf(TOK, W), buf(TOK, W), buf(W, TOK), buf(W, TOK),
        buf(8, 2, 128, TOK), buf(8, 128, TOK), buf(2, 64, TOK), buf(64, TOK),
        buf(3, 64, TOK), buf(3, 64, TOK), buf(2, 64, TOK),
        *sums(128, 80, TOK),
        buf(8, CH, TOK), buf(8, CH, TOK), *sums(256, 144, TOK),
        buf(8, TOK, CH), buf(8, TOK, CH), *sums(512, 288, CH),
        buf(ND, CH, TOK), buf(ND, CH, TOK), buf(ND, 128, TOK), buf(QKV, TOK),
        buf(2, 64, TOK), buf(64, TOK), buf(3, 64, TOK), buf(3, 64, TOK),
        wide(W, TOK), wide(W, TOK), buf(TOK, W), buf(NT, ROWS, W),
        wide(TOK, 128), wide(NT, ROWS, 128), wide(8, W), wide(NT, 8, W), wide(ND, ROWS, 128),
    ]
    counts = [4, 8, 8, 8, 8, 16, 16, 8, 8]
    counts += [5, 5, 8, 8, 8, 8] + [17] * 6 + [3] * 4
    counts += [20] * 6 + [2, 16, 16, 8, 8, 8, 8, 8, 8, 16, 16]
    semaphores = [dma((n,)) for n in counts]
    return pl.pallas_call(
        kernel,
        out_shape=(
            jax.ShapeDtypeStruct((ROWS, W), BF),
            jax.ShapeDtypeStruct((4, W), F32),
            jax.ShapeDtypeStruct((W, QKV), BF),
            jax.ShapeDtypeStruct((1024, W), BF),
            jax.ShapeDtypeStruct((W, FF), BF),
            jax.ShapeDtypeStruct((FF, W), BF),
        ),
        in_specs=[vmem] * 8 + [hbm] * 4,
        out_specs=(vmem, vmem, hbm, hbm, hbm, hbm),
        scratch_shapes=buffers + semaphores,
        compiler_params=pltpu.CompilerParams(
            collective_id=0, has_side_effects=True, vmem_limit_bytes=60 * 2**20
        ),
        cost_estimate=pl.CostEstimate(flops=14 * 10**9, bytes_accessed=21 * 10**6, transcendentals=10**6),
        name="block_backward",
    )(
        block_input, cotangent, attn_gain[None], attn_bias[None], mlp_gain[None], mlp_bias[None],
        cosine, sine, w_qkv, w_out, w_up, w_down,
    )


def solution(mesh):
    return jax.shard_map(
        on_device,
        mesh=mesh,
        in_specs=(
            P("tensor", "dp"),
            P("tensor", "dp"),
            P("dp"),
            P("dp"),
            P("dp"),
            P("dp"),
            P("dp", "tensor"),
            P("tensor", "dp"),
            P("dp", "tensor"),
            P("tensor", "dp"),
        ),
        out_specs=(
            P("tensor", "dp"),
            P(None, "dp"),
            P("dp", "tensor"),
            P("tensor", "dp"),
            P("dp", "tensor"),
            P("tensor", "dp"),
        ),
        check_vma=False,
    )
```

time: 245 us -> 174 us (0.71); the launches traced: 241 us -> 173 us
  Pallas kernels: 226 us -> 158 us
    pallas_call x1, Pallas kernels: 226 us -> 158 us  [on_device(): pl.pallas_call(kernel, out_shape=(jax.ShapeDtypeStruct((ROWS, W), BF), ja...]
where the time goes in v2:
time: 174 us; the launch traced here: 173 us
  Pallas kernels  158 us (91%)
  local copies, waits for them, and re-layouts  13.3 us (8%)
    pallas_call x1, Pallas kernels, on_device(): pl.pallas_call(kernel, out_shape=(jax.ShapeDtypeStruct((ROWS, W), BF), ja...  158 us
    unnamed x10, local copies, waits for them, and re-layouts  13.3 us

profile of v2, /device:TPU:1, one launch (start us, length us, event | category | flops | bytes accessed | tf_op | source)
XLA Modules:
  0.0 173.4 jit_solution(8875734975678751624)
XLA Ops:
  0.7 0.3 multiply_sine_fusion
  1.0 0.7 pad_maximum_fusion
  1.7 158.4 %block_backward.1 = (bf16[64,512]{1,0:T(8,128)(2,1)}, f32[4,512]{1,0:T(4,128)}, bf16[512,1152]{1,0:T(8,128)(2,1)}, bf16[1024,512]{1,0:T(8,128)(2,1)}, bf16[512,4...) custom-call(bf16[64,512]{1,0:T(8,128)(2,1)} %x_loc.1, bf16[64,512]{1,0:T(8,128)(2,1)} %c_loc.1, f32[1,512]{1,0:T(1,128)} %bitcast.4, ...), custom_call_target="tpu_custom_call" | custom-call | flops 14000000000 | bytes 21000000 | tf_op jit(solution)/shard_map/block_backward/pallas_call | solution.py:764
  160.1 0.0 copy-start.1
  160.1 1.6 copy.22
  161.7 1.3 copy.23
  163.0 2.4 %copy.24 = bf16[512,1152]{1,0:T(8,128)(2,1)} copy(bf16[512,1152]{1,0:T(8,128)(2,1)} %get-tuple-element.18) | data formatting | bytes 2359296
  165.4 2.3 %copy.25 = bf16[1024,512]{1,0:T(8,128)(2,1)} copy(bf16[1024,512]{1,0:T(8,128)(2,1)} %get-tuple-element.19) | data formatting | bytes 2097152
  167.7 0.0 copy-done.1
  167.7 0.0 copy-start
  167.7 2.1 %copy.26 = bf16[512,4096]{1,0:T(8,128)(2,1)} copy(bf16[512,4096]{1,0:T(8,128)(2,1)S(1)} %copy-done.1) | data formatting | bytes 8388608
  169.8 1.6 copy-done
  171.4 2.0 %copy.27 = bf16[4096,512]{1,0:T(8,128)(2,1)} copy(bf16[4096,512]{1,0:T(8,128)(2,1)S(1)} %copy-done) | data formatting | bytes 8388608
  (2 shorter events, 0.0 us)
Async XLA Ops:
  160.1 7.6 %copy-start.1 = (bf16[512,4096]{1,0:T(8,128)(2,1)S(1)}, bf16[512,4096]{1,0:T(8,128)(2,1)}, u32[]{:S(2)}) copy-start(bf16[512,4096]{1,0:T(8,128)(2,1)} %get-tuple-element.20) | copy-start | bytes 12582916
  167.7 3.7 %copy-start = (bf16[4096,512]{1,0:T(8,128)(2,1)S(1)}, bf16[4096,512]{1,0:T(8,128)(2,1)}, u32[]{:S(2)}) copy-start(bf16[4096,512]{1,0:T(8,128)(2,1)} %get-tuple-element.21) | copy-start | bytes 12582916

commit v3 on v2

--- a/solution.py
+++ b/solution.py
@@ -228,6 +228,8 @@
     def step_three(self):
         self.wait(5, 6)
         self.give((1, 3), (1, 1))
+
+    def step_four(self):
         self.wait(7, 10, 11)
         self.give((1, 2))
 
@@ -237,6 +239,65 @@
         for plane in range(2):
             for j in range(4):
                 self.hand(plane, j, self.place.c).wait_send()
+
+
+class Spread:
+    def __init__(self, place, buf, send, recv):
+        self.place, self.buf, self.send, self.recv = place, buf, send, recv
+        up, down, side = place.y_up, place.y_down, place.half_side
+        own, left, right, far = (0, 0), (0, 3), (0, 1), (0, 2)
+        h_own, h_left, h_right, h_far = (1, 0), (1, 3), (1, 1), (1, 2)
+        mid = ROWS // 2
+        self.moves = (
+            (own, left, 0, ROWS, up),
+            (own, right, 0, ROWS, down),
+            (own, h_own, 0, ROWS, side),
+            (left, far, 0, mid, up),
+            (right, far, mid, ROWS, down),
+            (h_own, h_left, 0, ROWS, up),
+            (h_own, h_right, 0, ROWS, down),
+            (h_left, h_far, 0, mid, up),
+            (h_right, h_far, mid, ROWS, down),
+        )
+
+    def copy(self, where, low, high, k, device):
+        first = pl.multiple_of(self.place.block(*where) * ROWS + low, 32)
+        at = self.buf.at[pl.ds(first, high - low)]
+        return self.place.remote(at, at, self.send.at[k], self.recv.at[k], device)
+
+    def go(self, *moves):
+        for k in moves:
+            src, _, low, high, device = self.moves[k]
+            self.copy(src, low, high, k, device).start()
+
+    def wait(self, *moves):
+        for k in moves:
+            _, dst, low, high, device = self.moves[k]
+            self.copy(dst, low, high, k, device).wait_recv()
+
+    def start(self):
+        self.go(2, 0, 1)
+
+    def step_one(self):
+        self.wait(2)
+        self.go(5, 6)
+        self.wait(0)
+        self.go(3)
+        self.wait(1)
+        self.go(4)
+
+    def step_two(self):
+        self.wait(5)
+        self.go(7)
+        self.wait(6)
+        self.go(8)
+
+    def step_three(self):
+        self.wait(3, 4, 7, 8)
+
+    def drain(self):
+        for k, (src, _, low, high, device) in enumerate(self.moves):
+            self.copy(src, low, high, k, device).wait_send()
 
 
 class Place:
@@ -253,6 +314,14 @@
         self.z_side = ((1 - z) * 8 + x * 2 + self.c, t)
         self.x_even = (z * 8 + (x + 1 - 2 * (x % 2)) * 2 + self.c, t)
         self.x_odd = (z * 8 + ((x + 3 + 2 * (x % 2)) % 4) * 2 + self.c, t)
+        self.y = y = t // 2
+        self.half = half = t % 2
+        self.y_up = (d, ((y + 1) % 4) * 2 + half)
+        self.y_down = (d, ((y + 3) % 4) * 2 + half)
+        self.half_side = (d, y * 2 + 1 - half)
+
+    def block(self, plane, j):
+        return ((self.y + j) % 4) * 2 + (self.half + plane) % 2
 
     def chip(self, plane, j):
         return ((self.z + plane) % 2) * 4 + (self.x + j) % 4
@@ -300,7 +369,7 @@
     d_out, d_in, d_part, d_z, d_1, d_2m, d_2p, d_f,
     h_out, h_in, h_part, h_z, h_1, h_2m, h_2p, h_f,
     act, hid, hq, proj, pp, pp_in, ppo, ppi,
-    abt, mbt, ngb, ngr, mom, momr, nrm, nrmr, m2,
+    abt, mbt, ngb, ngr, mom, momr, nrm, nrmr, m2, nrmd, ga, turned,
     w_sem, x_s, x_r, c_s, c_r, st_s, st_r, tt_s, tt_r,
     p_s, p_r, dp_s, dp_r, hp_s, hp_r, ts, tr, ds, dr, hs, hr, kv_s, kv_r, pp_s, pp_r,
     as_, ar, gs, gr, qs, qr, o_sem, u_sem, d_sem,
@@ -339,40 +408,50 @@
 
     own = rows(t, ROWS)
 
-    def send_c(k):
-        return remote(c_loc, cs.at[own], c_s.at[k], c_r.at[k], (d, (t + k) % NT))
-
-    def send_x(k):
-        return remote(x_loc, xs.at[own], x_s.at[k], x_r.at[k], (d, (t + k) % NT))
-
     def send_st(k):
         return remote(st_in.at[0], st_in.at[k], st_s.at[k], st_r.at[k], ((d + k) % ND, t))
 
     def send_tt(k):
-        return remote(st.at[own], st.at[own], tt_s.at[k], tt_r.at[k], (d, (t + k) % NT))
-
-    loop(1, NT, lambda k: send_c(k).start())
-    lane = lax.broadcasted_iota(jnp.int32, (ROWS, 128), 1)
+        return remote(st.at[t], st.at[t], tt_s.at[k], tt_r.at[k], (d, (t + k) % NT))
+
+    def wait_tt(k):
+        p = (t + NT - k) % NT
+        remote(st.at[p], st.at[p], tt_s.at[k], tt_r.at[k], (d, (t + k) % NT)).wait_recv()
+
+    spread_c = Spread(place, cs, c_s, c_r)
+    spread_x = Spread(place, xs, x_s, x_r)
+    cs[own, :] = c_loc[...]
+    spread_c.start()
+    xs[own, :] = x_loc[...]
+    spread_x.start()
+    lane = lax.broadcasted_iota(jnp.int32, (128, 128), 1)
+
+    def in_rows(one, two):
+        return jnp.where(lane < 4, one, two).T[0:8]
+
     xf = x_loc[...].astype(F32)
-    st_in[0] = jnp.where(
-        lane < 64, jnp.sum(xf, 1, keepdims=True), jnp.sum(xf * xf, 1, keepdims=True)
+    pad = jnp.zeros((ROWS, 1), F32)
+    st_in[0] = in_rows(
+        jnp.concatenate([jnp.sum(xf, 1, keepdims=True), pad], 0),
+        jnp.concatenate([jnp.sum(xf * xf, 1, keepdims=True), pad], 0),
     )
     loop(1, ND, lambda k: send_st(k).start())
-    cs[own, :] = c_loc[...]
-    xs[own, :] = x_loc[...]
-    weights[1].wait()
-    for i in range(QKV // 128):
-        wqt[i * 128 : (i + 1) * 128, :] = wq[:, i * 128 : (i + 1) * 128].T
+    spread_c.step_one()
+    spread_x.step_one()
     loop(1, ND, lambda k: send_st(k).wait_recv())
     total = st_in[0]
     for k in range(1, ND):
         total = total + st_in[k]
-    st[own, :] = total
+    st[t] = total
     loop(1, NT, lambda k: send_tt(k).start())
-    loop(1, NT, lambda k: send_c(k).wait_recv())
-    loop(1, NT, lambda k: send_x(k).start())
-
-    def produce(chunk, job, out, into, send, recv):
+    spread_c.step_two()
+    spread_x.step_two()
+    weights[1].wait()
+    for i in range(QKV // 128):
+        wqt[i * 128 : (i + 1) * 128, :] = wq[:, i * 128 : (i + 1) * 128].T
+    spread_c.step_three()
+
+    def produce(chunk, job, out, into, send, recv, hook):
         def pair(q, k):
             return remote(out.at[q], into.at[q], send.at[k], recv.at[k], partner)
 
@@ -402,6 +481,8 @@
             def _():
                 job.start()
 
+            hook(i)
+
         loop(0, 5, body)
 
     def pair_drain(out, into, send, recv):
@@ -411,31 +492,38 @@
     up = Reduce(place, h_part, h_z, h_1, h_2m, h_2p, h_f, hs, hr, (512, 288, 160, 384))
     attn = Reduce(place, t_part, t_z, t_1, t_2m, t_2p, t_f, ts, tr, (128, 80, 48, 96))
     weights[0].wait()
-    produce(lambda p: dot_nt(wd[rows(p, CH), :], cs[...]), down, d_out, d_in, dp_s, dp_r)
-
-    loop(1, NT, lambda k: send_x(k).wait_recv())
-    loop(1, NT, lambda k: send_tt(k).wait_recv())
-
-    def norm_rows(block, size):
-        here = rows(block, size)
-        average = st[here, 0:1] * (1.0 / D)
-        spread = st[here, 64:65] * (1.0 / D) - average * average
-        inverse = lax.rsqrt(spread + 1e-05)
-        return (xs[here, :].astype(F32) - average) * inverse, inverse
+    produce(
+        lambda p: dot_nt(wd[rows(p, CH), :], cs[...]), down, d_out, d_in, dp_s, dp_r, lambda i: None
+    )
+
+    weights[2].wait()
+
+    def og_body(i):
+        og = dot_nt(wo[rows(i, 256), :], cs[...]).astype(BF)
+        pa[pl.ds(i * 2, 2), :, 0:64, :] = og.reshape(2, 2, 64, TOK)
+
+    loop(0, 4, og_body)
+
+    spread_x.step_three()
+    loop(1, NT, wait_tt)
+
+    def scales(block):
+        columns = jnp.concatenate([st[block]] * 16, 0).T
+        average = columns[0:ROWS, 0:1] * (1.0 / D)
+        spread = columns[0:ROWS, 4:5] * (1.0 / D) - average * average
+        return average, lax.rsqrt(spread + 1e-05)
 
     def norm_body(block):
         here = rows(block, ROWS)
-        normed, _ = norm_rows(block, ROWS)
+        average, inverse = scales(block)
+        normed = (xs[here, :].astype(F32) - average) * inverse
+        nrmd[here, :] = normed
         ain[here, :] = (normed * ag[...] + ab[...]).astype(BF)
         min_[here, :] = (normed * mg[...] + mb[...]).astype(BF)
 
     loop(0, NT, norm_body)
 
-    weights[2].wait()
-
     def part_body(i):
-        og = dot_nt(wo[rows(i, 256), :], cs[...]).astype(BF)
-        pa[pl.ds(i * 2, 2), :, 0:64, :] = og.reshape(2, 2, 64, TOK)
         qq = dot_nt(wqt[rows(i, 256), :], ain[...]).astype(BF)
         pa[pl.ds(i * 2, 2), :, 64:128, :] = qq.reshape(2, 2, 64, TOK)
 
@@ -446,9 +534,9 @@
     give_a = remote(pa.at[:, other], pa_in, p_s.at[1], p_r.at[1], partner)
     give_a.start()
 
-    down.z_merge()
     down.step_two(1)
     down.step_two(0)
+    down.z_merge()
 
     kv_sum = Doubling(place, kvo, kvi, kv_s, kv_r)
     give_kv.wait_recv()
@@ -464,22 +552,32 @@
     attn.start()
 
     weights[3].wait()
-    produce(lambda p: dot_nn(min_[...], wu[:, rows(p, CH)]), up, h_out, h_in, hp_s, hp_r)
-
-    down.step_two(2)
-    down.step_z()
-    kv_sum.step(1)
+
+    def hook(i):
+        @pl.when(i == 2)
+        def _():
+            down.step_two(2)
+            kv_sum.step(1)
+
+        @pl.when(i == 3)
+        def _():
+            down.step_z()
+            attn.step_two(1)
+            attn.step_two(0)
+
+    produce(lambda p: dot_nn(min_[...], wu[:, rows(p, CH)]), up, h_out, h_in, hp_s, hp_r, hook)
+
     attn.z_merge()
-    attn.step_two(1)
-    attn.step_two(0)
     kv_sum.step(2)
-    up.z_merge()
     up.step_two(1)
     up.step_two(0)
     attn.step_two(2)
     attn.step_z()
     ain_t[...] = ain[...].T
     min_t[...] = min_[...].T
+    up.z_merge()
+    up.step_two(2)
+    up.step_z()
 
     attn.finish()
     og = attn.total(0, 64).astype(BF)
@@ -529,13 +627,9 @@
     give_pp = remote(pp.at[other], pp_in, p_s.at[3], p_r.at[3], partner)
     give_pp.start()
 
-    up.step_two(2)
-    up.step_z()
     give_pp.wait_recv()
     pp_sum = Doubling(place, ppo, ppi, pp_s, pp_r)
     pp_sum.start((pp[c].astype(F32) + pp_in[...].astype(F32)).astype(BF))
-    heads.step_one()
-    pp_sum.step(1)
     down.finish()
     up.finish()
 
@@ -551,10 +645,51 @@
     gather_hid = Gather(place, hid, gs, gr, (256, 144, 128, 80))
     gather_act.start()
     gather_hid.start()
-
+    mbt[...] = jnp.zeros((W, TOK), F32)
+
+    def out_d_copy(p):
+        return pltpu.make_async_copy(wd.at[rows(p, CH)], out_d.at[rows(p, CH)], d_sem.at[p])
+
+    def out_u_copy(p):
+        return pltpu.make_async_copy(wu.at[:, rows(p, CH)], out_u.at[:, rows(p, CH)], u_sem.at[p])
+
+    def use_act(plane, j):
+        def one(k):
+            p = place.chip(plane, j) * 2 + (c + k) % 2
+            wd[rows(p, CH), :] = dot_nn(act[p], cs[...]).astype(BF)
+            out_d_copy(p).start()
+
+        one(0)
+        gather_act.take(plane, j)
+        one(1)
+
+    def use_hid(plane, j):
+        def one(k):
+            p = place.chip(plane, j) * 2 + (c + k) % 2
+            mbt[...] += dot_nn(wu[:, rows(p, CH)], hid[p])
+            wu[:, rows(p, CH)] = dot_nt(min_t[...], hid[p]).astype(BF)
+            out_u_copy(p).start()
+
+        one(0)
+        gather_hid.take(plane, j)
+        one(1)
+
+    def near(f):
+        loop(0, 3, lambda i: f((3 - i) // 3, i + i // 2))
+
+    heads.step_one()
+    use_act(0, 0)
+    use_hid(0, 0)
+    pp_sum.step(1)
+
+    gather_act.step_one()
     heads.step_two()
     pp_sum.step(2)
+    near(use_act)
+
+    gather_hid.step_one()
     heads.step_three()
+    heads.step_four()
     there = rows(16 + c, 64)
     proj[there, :] = pp_sum.step(3).astype(BF)
     give_pj = remote(proj.at[there], proj.at[there], p_s.at[4], p_r.at[4], partner)
@@ -581,73 +716,31 @@
     out_q_copy = pltpu.make_async_copy(wq, out_q, o_sem.at[1])
     out_q_copy.start()
 
-    mbt[...] = jnp.zeros((W, TOK), F32)
-
-    def out_d_copy(p):
-        return pltpu.make_async_copy(wd.at[rows(p, CH)], out_d.at[rows(p, CH)], d_sem.at[p])
-
-    def out_u_copy(p):
-        return pltpu.make_async_copy(wu.at[:, rows(p, CH)], out_u.at[:, rows(p, CH)], u_sem.at[p])
-
-    def consume(p):
-        wd[rows(p, CH), :] = dot_nn(act[p], cs[...]).astype(BF)
-        out_d_copy(p).start()
-        mbt[...] += dot_nn(wu[:, rows(p, CH)], hid[p])
-        wu[:, rows(p, CH)] = dot_nt(min_t[...], hid[p]).astype(BF)
-        out_u_copy(p).start()
-
-    def ff_body(i):
-        @pl.when(i == 1)
-        def _():
-            gather_act.step_one()
-            gather_hid.step_one()
-
-        @pl.when(i == 3)
-        def _():
-            gather_act.step_two()
-            gather_hid.step_two()
-
-        @pl.when(i == 5)
-        def _():
-            gather_act.step_three()
-            gather_hid.step_three()
-
-        plane = i // 5 + (i + 6) // 7 - (i + 5) // 7
-        k = (i + 1) % 3
-        j = ((i + 1) // 3 + 1) // 2 * (1 + 2 * k - 3 * (k // 2))
-        consume(place.chip(plane, j) * 2 + c)
-        gather_act.take(plane, j)
-        gather_hid.take(plane, j)
-        consume(place.chip(plane, j) * 2 + other)
-
-    loop(0, 8, ff_body)
-
-    lane2 = lax.broadcasted_iota(jnp.int32, (128, 128), 1)
-
-    def tail_body(n):
+    gather_act.step_two()
+    near(use_hid)
+    gather_hid.step_two()
+
+    nrm[...] = jnp.zeros((8, W), F32)
+
+    def early_body(n):
         here = rows(n, 128)
         a_back = abt[:, here].T
-        m_back = mbt[:, here].T
-        normed, _ = norm_rows(n, 128)
-        grad = a_back * ag[...] + m_back * mg[...]
-        ngb[here, :] = grad.astype(BF)
-        mom[here, :] = jnp.where(
-            lane2 < 64, jnp.sum(grad, 1, keepdims=True), jnp.sum(grad * normed, 1, keepdims=True)
-        )
-        sums = jnp.concatenate(
-            [
-                jnp.sum(a_back * normed, 0, keepdims=True),
-                jnp.sum(a_back, 0, keepdims=True),
-                jnp.sum(m_back * normed, 0, keepdims=True),
-                jnp.sum(m_back, 0, keepdims=True),
-                jnp.zeros((4, W), F32),
-            ],
-            0,
-        )
-        nrm[...] += sums
-
-    nrm[...] = jnp.zeros((8, W), F32)
-    loop(0, 4, tail_body)
+        ga[here, :] = a_back * ag[...]
+        nrm[0:1, :] += jnp.sum(a_back * nrmd[here, :], 0, keepdims=True)
+        nrm[1:2, :] += jnp.sum(a_back, 0, keepdims=True)
+
+    loop(0, 4, early_body)
+
+    gather_act.step_three()
+    use_act(0, 2)
+    use_hid(0, 2)
+    gather_hid.step_three()
+    loop(0, 2, lambda i: use_act(1, 2 * i + 1))
+    gather_act.step_four()
+    loop(0, 2, lambda i: use_hid(1, 2 * i + 1))
+    gather_hid.step_four()
+    use_act(1, 2)
+    use_hid(1, 2)
 
     def send_ng(k):
         p = (t + k) % NT
@@ -655,19 +748,36 @@
 
     def send_mo(k):
         p = (t + k) % NT
-        return remote(mom.at[rows(p, ROWS)], momr.at[k], mo_s.at[k], mo_r.at[k], (d, p))
+        return remote(mom.at[p // 2], momr.at[k], mo_s.at[k], mo_r.at[k], (d, p))
 
     def send_nr(k):
         return remote(nrm, nrmr.at[k], nr_s.at[k], nr_r.at[k], (d, (t + k) % NT))
 
-    def start_tail(k):
-        send_mo(k).start()
-        send_ng(k).start()
-        send_nr(k).start()
-
-    loop(1, NT, start_tail)
+    def tail_body(i):
+        n = (t // 2 + 1 + i) % 4
+        here = rows(n, 128)
+        m_back = mbt[:, here].T
+        normed = nrmd[here, :]
+        grad = ga[here, :] + m_back * mg[...]
+        ngb[here, :] = grad.astype(BF)
+        mom[n] = in_rows(jnp.sum(grad, 1, keepdims=True), jnp.sum(grad * normed, 1, keepdims=True))
+        nrm[2:3, :] += jnp.sum(m_back * normed, 0, keepdims=True)
+        nrm[3:4, :] += jnp.sum(m_back, 0, keepdims=True)
+
+        def send(k):
+            @pl.when(k > 0)
+            def _():
+                send_mo(k).start()
+                send_ng(k).start()
+
+        send((2 * n - t + NT) % NT)
+        send((2 * n + 1 - t + NT) % NT)
+
+    loop(0, 4, tail_body)
+
+    loop(1, NT, lambda k: send_nr(k).start())
     loop(1, NT, lambda k: send_mo(k).wait_recv())
-    acc = mom[own, :]
+    acc = mom[t // 2]
     for k in range(1, NT):
         acc = acc + momr[k]
     m2[0] = acc
@@ -689,14 +799,16 @@
     moments = m2[0]
     for k in range(1, ND):
         moments = moments + m2[k]
-    first = moments[:, 0:1] * (1.0 / D)
-    second = moments[:, 64:65] * (1.0 / D)
-    normed, inverse = norm_rows(t, ROWS)
-    out_x[...] = (c_loc[...].astype(F32) + inverse * (grad - first - normed * second)).astype(BF)
+    turned[...] = jnp.concatenate([moments] * 16, 0).T
+    mine = turned[rows(t % 2, ROWS), :]
+    first = mine[:, 0:1] * (1.0 / D)
+    second = mine[:, 4:5] * (1.0 / D)
+    _, inverse = scales(t)
+    out_x[...] = (
+        c_loc[...].astype(F32) + inverse * (grad - first - nrmd[own, :] * second)
+    ).astype(BF)
 
     def drain_t(k):
-        send_c(k).wait_send()
-        send_x(k).wait_send()
         send_tt(k).wait_send()
         send_mo(k).wait_send()
         send_ng(k).wait_send()
@@ -716,7 +828,7 @@
         copy.wait_send()
     pair_drain(d_out, d_in, dp_s, dp_r)
     pair_drain(h_out, h_in, hp_s, hp_r)
-    for job in (down, up, attn, kv_sum, pp_sum, heads, gather_act, gather_hid):
+    for job in (spread_c, spread_x, down, up, attn, kv_sum, pp_sum, heads, gather_act, gather_hid):
         job.drain()
     out_o_copy.wait()
     out_q_copy.wait()
@@ -744,7 +856,7 @@
         ]
 
     buffers = [
-        buf(TOK, W), buf(TOK, W), wide(ND, ROWS, 128), wide(TOK, 128),
+        buf(TOK, W), buf(TOK, W), wide(ND, 8, 128), wide(NT, 8, 128),
         buf(W, QKV), buf(QKV, W), buf(1024, W), buf(W, FF), buf(FF, W),
         buf(TOK, W), buf(TOK, W), buf(W, TOK), buf(W, TOK),
         buf(8, 2, 128, TOK), buf(8, 128, TOK), buf(2, 64, TOK), buf(64, TOK),
@@ -755,9 +867,10 @@
         buf(ND, CH, TOK), buf(ND, CH, TOK), buf(ND, 128, TOK), buf(QKV, TOK),
         buf(2, 64, TOK), buf(64, TOK), buf(3, 64, TOK), buf(3, 64, TOK),
         wide(W, TOK), wide(W, TOK), buf(TOK, W), buf(NT, ROWS, W),
-        wide(TOK, 128), wide(NT, ROWS, 128), wide(8, W), wide(NT, 8, W), wide(ND, ROWS, 128),
+        wide(4, 8, 128), wide(NT, 8, 128), wide(8, W), wide(NT, 8, W), wide(ND, 8, 128),
+        wide(TOK, W), wide(TOK, W), wide(128, 128),
     ]
-    counts = [4, 8, 8, 8, 8, 16, 16, 8, 8]
+    counts = [4, 9, 9, 9, 9, 16, 16, 8, 8]
     counts += [5, 5, 8, 8, 8, 8] + [17] * 6 + [3] * 4
     counts += [20] * 6 + [2, 16, 16, 8, 8, 8, 8, 8, 8, 16, 16]
     semaphores = [dma((n,)) for n in counts]

time: 174 us -> 146 us (0.84)
  Pallas kernels: 158 us -> 131 us
    pallas_call x1, Pallas kernels: 158 us -> 131 us  [on_device(): pl.pallas_call(kernel, out_shape=(jax.ShapeDtypeStruct((ROWS, W), BF), ja...]
where the time goes in v3:
time: 146 us
  Pallas kernels  131 us (90%)
  local copies, waits for them, and re-layouts  13.3 us (9%)
    pallas_call x1, Pallas kernels, on_device(): pl.pallas_call(kernel, out_shape=(jax.ShapeDtypeStruct((ROWS, W), BF), ja...  131 us
    unnamed x10, local copies, waits for them, and re-layouts  13.3 us

profile of v3, /device:TPU:1, one launch (start us, length us, event | category | flops | bytes accessed | tf_op | source)
XLA Modules:
  0.0 145.8 jit_solution(5808784809509695697)
XLA Ops:
  0.7 0.3 multiply_sine_fusion
  1.0 0.7 pad_maximum_fusion
  1.7 130.8 %block_backward.1 = (bf16[64,512]{1,0:T(8,128)(2,1)}, f32[4,512]{1,0:T(4,128)}, bf16[512,1152]{1,0:T(8,128)(2,1)}, bf16[1024,512]{1,0:T(8,128)(2,1)}, bf16[512,4...) custom-call(bf16[64,512]{1,0:T(8,128)(2,1)} %x_loc.1, bf16[64,512]{1,0:T(8,128)(2,1)} %c_loc.1, f32[1,512]{1,0:T(1,128)} %bitcast.4, ...), custom_call_target="tpu_custom_call" | custom-call | flops 14000000000 | bytes 21000000 | tf_op jit(solution)/shard_map/block_backward/pallas_call | solution.py:877
  132.5 0.0 copy-start.1
  132.5 1.6 %copy.22 = bf16[64,512]{1,0:T(8,128)(2,1)} copy(bf16[64,512]{1,0:T(8,128)(2,1)} %get-tuple-element.16) | data formatting | bytes 131072
  134.2 1.3 copy.23
  135.5 2.4 %copy.24 = bf16[512,1152]{1,0:T(8,128)(2,1)} copy(bf16[512,1152]{1,0:T(8,128)(2,1)} %get-tuple-element.18) | data formatting | bytes 2359296
  137.8 2.3 %copy.25 = bf16[1024,512]{1,0:T(8,128)(2,1)} copy(bf16[1024,512]{1,0:T(8,128)(2,1)} %get-tuple-element.19) | data formatting | bytes 2097152
  140.1 0.0 copy-done.1
  140.1 0.0 copy-start
  140.1 2.1 %copy.26 = bf16[512,4096]{1,0:T(8,128)(2,1)} copy(bf16[512,4096]{1,0:T(8,128)(2,1)S(1)} %copy-done.1) | data formatting | bytes 8388608
  142.2 1.6 %copy-done = bf16[4096,512]{1,0:T(8,128)(2,1)S(1)} copy-done((bf16[4096,512]{1,0:T(8,128)(2,1)S(1)}, bf16[4096,512]{1,0:T(8,128)(2,1)}, u32[]{:S(2)}) %copy-start) | copy-done | bytes 4194328
  143.8 2.0 %copy.27 = bf16[4096,512]{1,0:T(8,128)(2,1)} copy(bf16[4096,512]{1,0:T(8,128)(2,1)S(1)} %copy-done) | data formatting | bytes 8388608
  (2 shorter events, 0.0 us)
Async XLA Ops:
  132.5 7.6 %copy-start.1 = (bf16[512,4096]{1,0:T(8,128)(2,1)S(1)}, bf16[512,4096]{1,0:T(8,128)(2,1)}, u32[]{:S(2)}) copy-start(bf16[512,4096]{1,0:T(8,128)(2,1)} %get-tuple-element.20) | copy-start | bytes 12582916
  140.1 3.7 %copy-start = (bf16[4096,512]{1,0:T(8,128)(2,1)S(1)}, bf16[4096,512]{1,0:T(8,128)(2,1)}, u32[]{:S(2)}) copy-start(bf16[4096,512]{1,0:T(8,128)(2,1)} %get-tuple-element.21) | copy-start | bytes 12582916

commit v4 on v3

--- a/solution.py
+++ b/solution.py
@@ -3,6 +3,7 @@
 
 import jax
 import jax.numpy as jnp
+import numpy as np
 from jax import lax
 from jax.experimental import pallas as pl
 from jax.experimental.pallas import tpu as pltpu
@@ -39,12 +40,12 @@
 
 def rope_columns():
     halfway = HD // 2
-    position = (jnp.arange(TOK) % LENGTH).astype(F32)
-    frequency = 10000.0 ** (-2.0 * jnp.arange(halfway).astype(F32) / HD)
+    position = (np.arange(TOK) % LENGTH).astype(np.float32)
+    frequency = (10000.0 ** (-2.0 * np.arange(halfway) / HD)).astype(np.float32)
     angle = frequency[:, None] * position[None, :]
-    cosine = jnp.concatenate([jnp.cos(angle), jnp.cos(angle)], 0)
-    sine = jnp.concatenate([jnp.sin(angle), jnp.sin(angle)], 0)
-    return cosine, sine
+    cosine = np.concatenate([np.cos(angle), np.cos(angle)], 0).astype(np.float32)
+    sine = np.concatenate([np.sin(angle), np.sin(angle)], 0).astype(np.float32)
+    return jnp.asarray(cosine), jnp.asarray(sine)
 
 
 def rotate(v, cosine, sine):
@@ -362,8 +363,8 @@
 
 def kernel(
     x_loc, c_loc, ag, ab, mg, mb, cosine, sine, wq_hbm, wo_hbm, wu_hbm, wd_hbm,
-    out_x, out_n, out_q, out_o, out_u, out_d,
-    xs, cs, st_in, st, wq, wqt, wo, wu, wd, ain, min_, ain_t, min_t,
+    out_x, out_n, wq, wo, wu, wd,
+    xs, cs, st_in, st, wqt, ain, min_, ain_t, min_t,
     pa, pa_in, pkv, pkv_in, kvo, kvi, kvx,
     t_part, t_z, t_1, t_2m, t_2p, t_f,
     d_out, d_in, d_part, d_z, d_1, d_2m, d_2p, d_f,
@@ -372,7 +373,7 @@
     abt, mbt, ngb, ngr, mom, momr, nrm, nrmr, m2, nrmd, ga, turned,
     w_sem, x_s, x_r, c_s, c_r, st_s, st_r, tt_s, tt_r,
     p_s, p_r, dp_s, dp_r, hp_s, hp_r, ts, tr, ds, dr, hs, hr, kv_s, kv_r, pp_s, pp_r,
-    as_, ar, gs, gr, qs, qr, o_sem, u_sem, d_sem,
+    as_, ar, gs, gr, qs, qr,
     ng_s, ng_r, mo_s, mo_r, nr_s, nr_r, m2_s, m2_r,
 ):
     place = Place()
@@ -404,26 +405,10 @@
         1, ND,
         lambda k: pl.semaphore_signal(barrier, inc=1, device_id=((d + k) % ND, t), device_id_type=MESH),
     )
-    pl.semaphore_wait(barrier, NT - 1 + ND - 1)
 
     own = rows(t, ROWS)
-
-    def send_st(k):
-        return remote(st_in.at[0], st_in.at[k], st_s.at[k], st_r.at[k], ((d + k) % ND, t))
-
-    def send_tt(k):
-        return remote(st.at[t], st.at[t], tt_s.at[k], tt_r.at[k], (d, (t + k) % NT))
-
-    def wait_tt(k):
-        p = (t + NT - k) % NT
-        remote(st.at[p], st.at[p], tt_s.at[k], tt_r.at[k], (d, (t + k) % NT)).wait_recv()
-
-    spread_c = Spread(place, cs, c_s, c_r)
-    spread_x = Spread(place, xs, x_s, x_r)
     cs[own, :] = c_loc[...]
-    spread_c.start()
     xs[own, :] = x_loc[...]
-    spread_x.start()
     lane = lax.broadcasted_iota(jnp.int32, (128, 128), 1)
 
     def in_rows(one, two):
@@ -435,7 +420,26 @@
         jnp.concatenate([jnp.sum(xf, 1, keepdims=True), pad], 0),
         jnp.concatenate([jnp.sum(xf * xf, 1, keepdims=True), pad], 0),
     )
+    pl.semaphore_wait(barrier, NT - 1 + ND - 1)
+
+    def send_st(k):
+        return remote(st_in.at[0], st_in.at[k], st_s.at[k], st_r.at[k], ((d + k) % ND, t))
+
+    def send_tt(k):
+        return remote(st.at[t], st.at[t], tt_s.at[k], tt_r.at[k], (d, (t + k) % NT))
+
+    def wait_tt(k):
+        p = (t + NT - k) % NT
+        remote(st.at[p], st.at[p], tt_s.at[k], tt_r.at[k], (d, (t + k) % NT)).wait_recv()
+
+    spread_c = Spread(place, cs, c_s, c_r)
+    spread_x = Spread(place, xs, x_s, x_r)
+    spread_c.start()
+    spread_x.start()
     loop(1, ND, lambda k: send_st(k).start())
+    weights[1].wait()
+    for i in range(QKV // 128):
+        wqt[i * 128 : (i + 1) * 128, :] = wq[:, i * 128 : (i + 1) * 128].T
     spread_c.step_one()
     spread_x.step_one()
     loop(1, ND, lambda k: send_st(k).wait_recv())
@@ -446,9 +450,6 @@
     loop(1, NT, lambda k: send_tt(k).start())
     spread_c.step_two()
     spread_x.step_two()
-    weights[1].wait()
-    for i in range(QKV // 128):
-        wqt[i * 128 : (i + 1) * 128, :] = wq[:, i * 128 : (i + 1) * 128].T
     spread_c.step_three()
 
     def produce(chunk, job, out, into, send, recv, hook):
@@ -571,11 +572,14 @@
     kv_sum.step(2)
     up.step_two(1)
     up.step_two(0)
+
     attn.step_two(2)
     attn.step_z()
     ain_t[...] = ain[...].T
     min_t[...] = min_[...].T
+
     up.z_merge()
+
     up.step_two(2)
     up.step_z()
 
@@ -647,17 +651,10 @@
     gather_hid.start()
     mbt[...] = jnp.zeros((W, TOK), F32)
 
-    def out_d_copy(p):
-        return pltpu.make_async_copy(wd.at[rows(p, CH)], out_d.at[rows(p, CH)], d_sem.at[p])
-
-    def out_u_copy(p):
-        return pltpu.make_async_copy(wu.at[:, rows(p, CH)], out_u.at[:, rows(p, CH)], u_sem.at[p])
-
     def use_act(plane, j):
         def one(k):
             p = place.chip(plane, j) * 2 + (c + k) % 2
             wd[rows(p, CH), :] = dot_nn(act[p], cs[...]).astype(BF)
-            out_d_copy(p).start()
 
         one(0)
         gather_act.take(plane, j)
@@ -668,7 +665,6 @@
             p = place.chip(plane, j) * 2 + (c + k) % 2
             mbt[...] += dot_nn(wu[:, rows(p, CH)], hid[p])
             wu[:, rows(p, CH)] = dot_nt(min_t[...], hid[p]).astype(BF)
-            out_u_copy(p).start()
 
         one(0)
         gather_hid.take(plane, j)
@@ -681,13 +677,15 @@
     use_act(0, 0)
     use_hid(0, 0)
     pp_sum.step(1)
-
-    gather_act.step_one()
     heads.step_two()
     pp_sum.step(2)
+
+    gather_act.step_one()
+    gather_hid.step_one()
+
     near(use_act)
-
-    gather_hid.step_one()
+    near(use_hid)
+
     heads.step_three()
     heads.step_four()
     there = rows(16 + c, 64)
@@ -705,19 +703,14 @@
         proj[rows(i, 256), :] = hq[pl.ds(i * 4, 4), 64:128, :].reshape(256, TOK)
 
     loop(0, 4, go_body)
-    out_o_copy = pltpu.make_async_copy(wo, out_o, o_sem.at[0])
-    out_o_copy.start()
 
     def ab_body(i):
         abt[rows(i, 128), :] = dot_nn(wq[rows(i, 128), :], proj[...])
         wq[rows(i, 128), :] = dot_nt(ain_t[rows(i, 128), :], proj[...]).astype(BF)
 
     loop(0, 4, ab_body)
-    out_q_copy = pltpu.make_async_copy(wq, out_q, o_sem.at[1])
-    out_q_copy.start()
 
     gather_act.step_two()
-    near(use_hid)
     gather_hid.step_two()
 
     nrm[...] = jnp.zeros((8, W), F32)
@@ -731,13 +724,13 @@
 
     loop(0, 4, early_body)
 
-    gather_act.step_three()
     use_act(0, 2)
     use_hid(0, 2)
+    gather_act.step_three()
     gather_hid.step_three()
     loop(0, 2, lambda i: use_act(1, 2 * i + 1))
+    loop(0, 2, lambda i: use_hid(1, 2 * i + 1))
     gather_act.step_four()
-    loop(0, 2, lambda i: use_hid(1, 2 * i + 1))
     gather_hid.step_four()
     use_act(1, 2)
     use_hid(1, 2)
@@ -818,10 +811,6 @@
         send_st(k).wait_send()
         send_m2(k).wait_send()
 
-    def drain_o(p):
-        out_d_copy(p).wait()
-        out_u_copy(p).wait()
-
     loop(1, NT, drain_t)
     loop(1, ND, drain_d)
     for copy in (give_a, give_kv, give, give_pp, give_pj):
@@ -830,9 +819,14 @@
     pair_drain(h_out, h_in, hp_s, hp_r)
     for job in (spread_c, spread_x, down, up, attn, kv_sum, pp_sum, heads, gather_act, gather_hid):
         job.drain()
-    out_o_copy.wait()
-    out_q_copy.wait()
-    loop(0, ND, drain_o)
+
+
+def write_out(*refs):
+    copies = [pltpu.make_async_copy(refs[i], refs[6 + i], refs[12].at[i]) for i in range(6)]
+    for copy in copies:
+        copy.start()
+    for copy in copies:
+        copy.wait()
 
 
 def on_device(
@@ -857,7 +851,7 @@
 
     buffers = [
         buf(TOK, W), buf(TOK, W), wide(ND, 8, 128), wide(NT, 8, 128),
-        buf(W, QKV), buf(QKV, W), buf(1024, W), buf(W, FF), buf(FF, W),
+        buf(QKV, W),
         buf(TOK, W), buf(TOK, W), buf(W, TOK), buf(W, TOK),
         buf(8, 2, 128, TOK), buf(8, 128, TOK), buf(2, 64, TOK), buf(64, TOK),
         buf(3, 64, TOK), buf(3, 64, TOK), buf(2, 64, TOK),
@@ -872,23 +866,23 @@
     ]
     counts = [4, 9, 9, 9, 9, 16, 16, 8, 8]
     counts += [5, 5, 8, 8, 8, 8] + [17] * 6 + [3] * 4
-    counts += [20] * 6 + [2, 16, 16, 8, 8, 8, 8, 8, 8, 16, 16]
+    counts += [20] * 6 + [8, 8, 8, 8, 8, 8, 16, 16]
     semaphores = [dma((n,)) for n in counts]
-    return pl.pallas_call(
+    results = pl.pallas_call(
         kernel,
         out_shape=(
-            jax.ShapeDtypeStruct((ROWS, W), BF),
-            jax.ShapeDtypeStruct((4, W), F32),
-            jax.ShapeDtypeStruct((W, QKV), BF),
-            jax.ShapeDtypeStruct((1024, W), BF),
-            jax.ShapeDtypeStruct((W, FF), BF),
-            jax.ShapeDtypeStruct((FF, W), BF),
+            pltpu.VMEM((ROWS, W), BF),
+            pltpu.VMEM((4, W), F32),
+            pltpu.VMEM((W, QKV), BF),
+            pltpu.VMEM((1024, W), BF),
+            pltpu.VMEM((W, FF), BF),
+            pltpu.VMEM((FF, W), BF),
         ),
         in_specs=[vmem] * 8 + [hbm] * 4,
-        out_specs=(vmem, vmem, hbm, hbm, hbm, hbm),
+        out_specs=(vmem,) * 6,
         scratch_shapes=buffers + semaphores,
         compiler_params=pltpu.CompilerParams(
-            collective_id=0, has_side_effects=True, vmem_limit_bytes=60 * 2**20
+            collective_id=0, has_side_effects=True, vmem_limit_bytes=46 * 2**20
         ),
         cost_estimate=pl.CostEstimate(flops=14 * 10**9, bytes_accessed=21 * 10**6, transcendentals=10**6),
         name="block_backward",
@@ -896,6 +890,15 @@
         block_input, cotangent, attn_gain[None], attn_bias[None], mlp_gain[None], mlp_bias[None],
         cosine, sine, w_qkv, w_out, w_up, w_down,
     )
+    return pl.pallas_call(
+        write_out,
+        out_shape=tuple(jax.ShapeDtypeStruct(r.shape, r.dtype) for r in results),
+        in_specs=[vmem] * 6,
+        out_specs=(hbm,) * 6,
+        scratch_shapes=[dma((6,))],
+        compiler_params=pltpu.CompilerParams(vmem_limit_bytes=4 * 2**20),
+        name="write_results",
+    )(*[pltpu.with_memory_space_constraint(r, pltpu.VMEM) for r in results])
 
 
 def solution(mesh):

time: 146 us -> 137 us (0.938)
  local copies, waits for them, and re-layouts: 13.3 us -> 0 us
  Pallas kernels: 131 us -> 136 us
    unnamed x10 -> x0, local copies, waits for them, and re-layouts: 13.3 us -> none
    pallas_call x1 -> x2, Pallas kernels: 131 us -> 136 us  [the longest x1 132 us: on_device(): pl.pallas_call(kernel, out_shape=(pltpu.VMEM((ROWS, W), BF), pltpu.VMEM((...]
where the time goes in v4:
time: 137 us
  Pallas kernels  136 us (99%)
    pallas_call x1, Pallas kernels, on_device(): pl.pallas_call(kernel, out_shape=(pltpu.VMEM((ROWS, W), BF), pltpu.VMEM((...  132 us
    pallas_call x1, Pallas kernels, on_device(): pl.pallas_call(write_out, out_shape=tuple((jax.ShapeDtypeStruct(r.shape,...  4.21 us

profile of v4, /device:TPU:1, one launch (start us, length us, event | category | flops | bytes accessed | tf_op | source)
XLA Modules:
  0.0 137.0 jit_solution(14219159879293412564)
XLA Ops:
  0.6 132.0 %block_backward.1 = (bf16[64,512]{1,0:T(8,128)(2,1)S(1)}, f32[4,512]{1,0:T(4,128)S(1)}, bf16[512,1152]{1,0:T(8,128)(2,1)S(1)}, bf16[1024,512]{1,0:T(8,128)(2,1)S...) custom-call(bf16[64,512]{1,0:T(8,128)(2,1)} %x_loc.1, bf16[64,512]{1,0:T(8,128)(2,1)} %c_loc.1, ...), custom_call_target="tpu_custom_call" | custom-call | flops 14000000000 | bytes 21000000 | tf_op jit(solution)/shard_map/block_backward/pallas_call | solution.py:871
  132.7 4.2 %write_results.1 = (bf16[64,512]{1,0:T(8,128)(2,1)}, f32[4,512]{1,0:T(4,128)}, bf16[512,1152]{1,0:T(8,128)(2,1)}, bf16[1024,512]{1,0:T(8,128)(2,1)}, bf16[512,40...) custom-call(bf16[64,512]{1,0:T(8,128)(2,1)S(1)} %get-tuple-element.12.refs_0_, f32[4,512]{1,0:T(4,128)S(1)} %get-tuple-element.13.refs_1_, ...), custom_call_target="tpu_custom_call" | custom-call | tf_op jit(solution)/shard_map/write_results/pallas_call | solution.py:893

commit v5 on v4

--- a/solution.py
+++ b/solution.py
@@ -366,9 +366,9 @@
     out_x, out_n, wq, wo, wu, wd,
     xs, cs, st_in, st, wqt, ain, min_, ain_t, min_t,
     pa, pa_in, pkv, pkv_in, kvo, kvi, kvx,
-    t_part, t_z, t_1, t_2m, t_2p, t_f,
-    d_out, d_in, d_part, d_z, d_1, d_2m, d_2p, d_f,
-    h_out, h_in, h_part, h_z, h_1, h_2m, h_2p, h_f,
+    t_z, t_1, t_2m, t_2p, t_f,
+    d_out, d_in, d_z, d_1, d_2m, d_2p, d_f,
+    h_out, h_in, h_z, h_1, h_2m, h_2p, h_f,
     act, hid, hq, proj, pp, pp_in, ppo, ppi,
     abt, mbt, ngb, ngr, mom, momr, nrm, nrmr, m2, nrmd, ga, turned,
     w_sem, x_s, x_r, c_s, c_r, st_s, st_r, tt_s, tt_r,
@@ -432,29 +432,31 @@
         p = (t + NT - k) % NT
         remote(st.at[p], st.at[p], tt_s.at[k], tt_r.at[k], (d, (t + k) % NT)).wait_recv()
 
-    spread_c = Spread(place, cs, c_s, c_r)
+    def send_c(k):
+        return remote(cs.at[own], cs.at[own], c_s.at[k], c_r.at[k], (d, (t + k) % NT))
+
+    def wait_c(k):
+        there = rows((t + NT - k) % NT, ROWS)
+        remote(cs.at[there], cs.at[there], c_s.at[k], c_r.at[k], (d, (t + k) % NT)).wait_recv()
+
     spread_x = Spread(place, xs, x_s, x_r)
-    spread_c.start()
-    spread_x.start()
+    loop(1, NT, lambda k: send_c(k).start())
     loop(1, ND, lambda k: send_st(k).start())
     weights[1].wait()
     for i in range(QKV // 128):
         wqt[i * 128 : (i + 1) * 128, :] = wq[:, i * 128 : (i + 1) * 128].T
-    spread_c.step_one()
-    spread_x.step_one()
     loop(1, ND, lambda k: send_st(k).wait_recv())
     total = st_in[0]
     for k in range(1, ND):
         total = total + st_in[k]
     st[t] = total
     loop(1, NT, lambda k: send_tt(k).start())
-    spread_c.step_two()
-    spread_x.step_two()
-    spread_c.step_three()
-
-    def produce(chunk, job, out, into, send, recv, hook):
+    loop(1, NT, wait_c)
+    spread_x.start()
+
+    def produce(both, job, out, into, send, recv, hook):
         def pair(q, k):
-            return remote(out.at[q], into.at[q], send.at[k], recv.at[k], partner)
+            return remote(out.at[q, other], into.at[q], send.at[k], recv.at[k], partner)
 
         def body(i):
             @pl.when(i < 4)
@@ -462,11 +464,8 @@
                 j = (2 + 3 * i) % 4
                 for plane in (1, 0):
                     q = place.chip(plane, j)
-                    out[q] = chunk(2 * q + other).astype(BF)
+                    out[q, 0], out[q, 1] = both(q)
                     pair(q, 2 * i + plane).start()
-                for plane in (1, 0):
-                    q = place.chip(plane, j)
-                    job.part[q] = chunk(2 * q + c).astype(BF)
 
             @pl.when(i > 0)
             def _():
@@ -474,7 +473,7 @@
                 for plane in (1, 0):
                     q = place.chip(plane, j)
                     pair(q, 2 * (i - 1) + plane).wait_recv()
-                    job.part[q] = (job.part[q].astype(F32) + into[q].astype(F32)).astype(BF)
+                    job.part[q] = (out[q, c].astype(F32) + into[q].astype(F32)).astype(BF)
                     if plane == 1:
                         job.z_first(j).start()
 
@@ -487,15 +486,33 @@
         loop(0, 5, body)
 
     def pair_drain(out, into, send, recv):
-        loop(0, 8, lambda k: remote(out.at[k], into.at[k], send.at[k], recv.at[k], partner).wait_send())
-
-    down = Reduce(place, d_part, d_z, d_1, d_2m, d_2p, d_f, ds, dr, (256, 144, 80, 192))
-    up = Reduce(place, h_part, h_z, h_1, h_2m, h_2p, h_f, hs, hr, (512, 288, 160, 384))
-    attn = Reduce(place, t_part, t_z, t_1, t_2m, t_2p, t_f, ts, tr, (128, 80, 48, 96))
+        loop(0, 8, lambda k: remote(out.at[k, other], into.at[k], send.at[k], recv.at[k], partner).wait_send())
+
+    down = Reduce(place, d_in, d_z, d_1, d_2m, d_2p, d_f, ds, dr, (256, 144, 80, 192))
+    up = Reduce(place, h_in, h_z, h_1, h_2m, h_2p, h_f, hs, hr, (512, 288, 160, 384))
+    attn = Reduce(place, pa_in, t_z, t_1, t_2m, t_2p, t_f, ts, tr, (128, 80, 48, 96))
     weights[0].wait()
-    produce(
-        lambda p: dot_nt(wd[rows(p, CH), :], cs[...]), down, d_out, d_in, dp_s, dp_r, lambda i: None
-    )
+
+    def down_both(q):
+        two = dot_nt(wd[rows(q, 2 * CH), :], cs[...]).astype(BF)
+        return two[:CH], two[CH:]
+
+    def up_both(q):
+        two = dot_nn(min_[...], wu[:, rows(q, 2 * CH)]).astype(BF)
+        return two[:, :CH], two[:, CH:]
+
+    def down_hook(i):
+        @pl.when(i == 3)
+        def _():
+            spread_x.step_one()
+
+        @pl.when(i == 4)
+        def _():
+            down.step_two(1)
+            down.step_two(0)
+            spread_x.step_two()
+
+    produce(down_both, down, d_out, d_in, dp_s, dp_r, down_hook)
 
     weights[2].wait()
 
@@ -524,6 +541,8 @@
 
     loop(0, NT, norm_body)
 
+    down.z_merge()
+
     def part_body(i):
         qq = dot_nt(wqt[rows(i, 256), :], ain[...]).astype(BF)
         pa[pl.ds(i * 2, 2), :, 64:128, :] = qq.reshape(2, 2, 64, TOK)
@@ -535,53 +554,54 @@
     give_a = remote(pa.at[:, other], pa_in, p_s.at[1], p_r.at[1], partner)
     give_a.start()
 
-    down.step_two(1)
-    down.step_two(0)
-    down.z_merge()
-
     kv_sum = Doubling(place, kvo, kvi, kv_s, kv_r)
     give_kv.wait_recv()
     kv_sum.start((pkv[c].astype(F32) + pkv_in[...].astype(F32)).astype(BF))
     give_a.wait_recv()
 
     def sum_a(q):
-        t_part[q] = (pa[q, c].astype(F32) + pa_in[q].astype(F32)).astype(BF)
+        pa_in[q] = (pa[q, c].astype(F32) + pa_in[q].astype(F32)).astype(BF)
 
     loop(0, 8, sum_a)
     for j in (2, 1, 0, 3):
         attn.z_first(j).start()
     attn.start()
 
+    down.step_two(2)
+
     weights[3].wait()
 
     def hook(i):
         @pl.when(i == 2)
         def _():
-            down.step_two(2)
-            kv_sum.step(1)
+            down.step_z()
 
         @pl.when(i == 3)
         def _():
-            down.step_z()
+            kv_sum.step(1)
+
+        @pl.when(i == 4)
+        def _():
             attn.step_two(1)
             attn.step_two(0)
 
-    produce(lambda p: dot_nn(min_[...], wu[:, rows(p, CH)]), up, h_out, h_in, hp_s, hp_r, hook)
+    produce(up_both, up, h_out, h_in, hp_s, hp_r, hook)
+
+    up.step_two(1)
+    up.step_two(0)
 
     attn.z_merge()
     kv_sum.step(2)
-    up.step_two(1)
-    up.step_two(0)
-
-    attn.step_two(2)
     attn.step_z()
     ain_t[...] = ain[...].T
     min_t[...] = min_[...].T
 
     up.z_merge()
+    up.step_z()
+
+    attn.step_two(2)
 
     up.step_two(2)
-    up.step_z()
 
     attn.finish()
     og = attn.total(0, 64).astype(BF)
@@ -648,43 +668,41 @@
     gather_act = Gather(place, act, as_, ar, (256, 144, 128, 80))
     gather_hid = Gather(place, hid, gs, gr, (256, 144, 128, 80))
     gather_act.start()
-    gather_hid.start()
+    gather_hid.give((0, 0))
     mbt[...] = jnp.zeros((W, TOK), F32)
 
     def use_act(plane, j):
-        def one(k):
-            p = place.chip(plane, j) * 2 + (c + k) % 2
-            wd[rows(p, CH), :] = dot_nn(act[p], cs[...]).astype(BF)
-
-        one(0)
+        q = place.chip(plane, j)
         gather_act.take(plane, j)
-        one(1)
+        wd[rows(q, 2 * CH), :] = dot_nn(act[pl.ds(2 * q, 2)].reshape(2 * CH, TOK), cs[...]).astype(BF)
+
+    def back_hid(plane, j):
+        q = place.chip(plane, j)
+        gather_hid.take(plane, j)
+        mbt[...] += dot_nn(wu[:, rows(q, 2 * CH)], hid[pl.ds(2 * q, 2)].reshape(2 * CH, TOK))
+
+    def grad_hid(plane, j):
+        q = place.chip(plane, j)
+        two = hid[pl.ds(2 * q, 2)].reshape(2 * CH, TOK)
+        wu[:, rows(q, 2 * CH)] = dot_nt(min_t[...], two).astype(BF)
 
     def use_hid(plane, j):
-        def one(k):
-            p = place.chip(plane, j) * 2 + (c + k) % 2
-            mbt[...] += dot_nn(wu[:, rows(p, CH)], hid[p])
-            wu[:, rows(p, CH)] = dot_nt(min_t[...], hid[p]).astype(BF)
-
-        one(0)
-        gather_hid.take(plane, j)
-        one(1)
+        back_hid(plane, j)
+        grad_hid(plane, j)
 
     def near(f):
         loop(0, 3, lambda i: f((3 - i) // 3, i + i // 2))
 
     heads.step_one()
+    pp_sum.step(1)
     use_act(0, 0)
     use_hid(0, 0)
-    pp_sum.step(1)
+
     heads.step_two()
+    gather_hid.go(0, 1, 2)
     pp_sum.step(2)
 
     gather_act.step_one()
-    gather_hid.step_one()
-
-    near(use_act)
-    near(use_hid)
 
     heads.step_three()
     heads.step_four()
@@ -705,13 +723,10 @@
     loop(0, 4, go_body)
 
     def ab_body(i):
-        abt[rows(i, 128), :] = dot_nn(wq[rows(i, 128), :], proj[...])
-        wq[rows(i, 128), :] = dot_nt(ain_t[rows(i, 128), :], proj[...]).astype(BF)
-
-    loop(0, 4, ab_body)
-
-    gather_act.step_two()
-    gather_hid.step_two()
+        abt[rows(i, 256), :] = dot_nn(wq[rows(i, 256), :], proj[...])
+        wq[rows(i, 256), :] = dot_nt(ain_t[rows(i, 256), :], proj[...]).astype(BF)
+
+    loop(0, 2, ab_body)
 
     nrm[...] = jnp.zeros((8, W), F32)
 
@@ -724,16 +739,23 @@
 
     loop(0, 4, early_body)
 
+    near(use_act)
+
+    gather_act.step_two()
+    gather_hid.step_one()
+
+    near(use_hid)
     use_act(0, 2)
+    gather_act.step_three()
+    gather_act.step_four()
+
+    gather_hid.step_two()
+
     use_hid(0, 2)
-    gather_act.step_three()
     gather_hid.step_three()
-    loop(0, 2, lambda i: use_act(1, 2 * i + 1))
-    loop(0, 2, lambda i: use_hid(1, 2 * i + 1))
-    gather_act.step_four()
+    loop(0, 2, lambda i: back_hid(1, 2 * i + 1))
     gather_hid.step_four()
-    use_act(1, 2)
-    use_hid(1, 2)
+    back_hid(1, 2)
 
     def send_ng(k):
         p = (t + k) % NT
@@ -769,6 +791,7 @@
     loop(0, 4, tail_body)
 
     loop(1, NT, lambda k: send_nr(k).start())
+    loop(1, 4, lambda i: grad_hid(1, i))
     loop(1, NT, lambda k: send_mo(k).wait_recv())
     acc = mom[t // 2]
     for k in range(1, NT):
@@ -779,6 +802,7 @@
         return remote(m2.at[0], m2.at[k], m2_s.at[k], m2_r.at[k], ((d + k) % ND, t))
 
     loop(1, ND, lambda k: send_m2(k).start())
+    loop(1, 4, lambda i: use_act(1, i))
     loop(1, NT, lambda k: send_ng(k).wait_recv())
     loop(1, NT, lambda k: send_nr(k).wait_recv())
     norm_total = nrm[...]
@@ -817,7 +841,8 @@
         copy.wait_send()
     pair_drain(d_out, d_in, dp_s, dp_r)
     pair_drain(h_out, h_in, hp_s, hp_r)
-    for job in (spread_c, spread_x, down, up, attn, kv_sum, pp_sum, heads, gather_act, gather_hid):
+    loop(1, NT, lambda k: send_c(k).wait_send())
+    for job in (spread_x, down, up, attn, kv_sum, pp_sum, heads, gather_act, gather_hid):
         job.drain()
 
 
@@ -845,7 +870,7 @@
 
     def sums(size, a, width):
         return [
-            buf(8, size, width), buf(4, size - a, width), buf(2, size, width),
+            buf(4, size - a, width), buf(2, size, width),
             buf(2, size, width), buf(2, size, width), buf(a, width),
         ]
 
@@ -856,8 +881,8 @@
         buf(8, 2, 128, TOK), buf(8, 128, TOK), buf(2, 64, TOK), buf(64, TOK),
         buf(3, 64, TOK), buf(3, 64, TOK), buf(2, 64, TOK),
         *sums(128, 80, TOK),
-        buf(8, CH, TOK), buf(8, CH, TOK), *sums(256, 144, TOK),
-        buf(8, TOK, CH), buf(8, TOK, CH), *sums(512, 288, CH),
+        buf(8, 2, CH, TOK), buf(8, CH, TOK), *sums(256, 144, TOK),
+        buf(8, 2, TOK, CH), buf(8, TOK, CH), *sums(512, 288, CH),
         buf(ND, CH, TOK), buf(ND, CH, TOK), buf(ND, 128, TOK), buf(QKV, TOK),
         buf(2, 64, TOK), buf(64, TOK), buf(3, 64, TOK), buf(3, 64, TOK),
         wide(W, TOK), wide(W, TOK), buf(TOK, W), buf(NT, ROWS, W),
@@ -882,7 +907,7 @@
         out_specs=(vmem,) * 6,
         scratch_shapes=buffers + semaphores,
         compiler_params=pltpu.CompilerParams(
-            collective_id=0, has_side_effects=True, vmem_limit_bytes=46 * 2**20
+            collective_id=0, has_side_effects=True, vmem_limit_bytes=48 * 2**20
         ),
         cost_estimate=pl.CostEstimate(flops=14 * 10**9, bytes_accessed=21 * 10**6, transcendentals=10**6),
         name="block_backward",

time: 137 us -> 134 us (0.978)
  Pallas kernels: 136 us -> 133 us
    pallas_call x1, Pallas kernels: 132 us -> 129 us  [on_device(): pl.pallas_call(kernel, out_shape=(pltpu.VMEM((ROWS, W), BF), pltpu.VMEM((...]
where the time goes in v5:
time: 134 us
  Pallas kernels  133 us (99%)
    pallas_call x1, Pallas kernels, on_device(): pl.pallas_call(kernel, out_shape=(pltpu.VMEM((ROWS, W), BF), pltpu.VMEM((...  129 us
    pallas_call x1, Pallas kernels, on_device(): pl.pallas_call(write_out, out_shape=tuple((jax.ShapeDtypeStruct(r.shape,...  4.21 us

profile of v5, /device:TPU:1, one launch (start us, length us, event | category | flops | bytes accessed | tf_op | source)
XLA Modules:
  0.0 134.0 jit_solution(11273757704265223294)
XLA Ops:
  0.6 129.1 %block_backward.1 = (bf16[64,512]{1,0:T(8,128)(2,1)S(1)}, f32[4,512]{1,0:T(4,128)S(1)}, bf16[512,1152]{1,0:T(8,128)(2,1)S(1)}, bf16[1024,512]{1,0:T(8,128)(2,1)S...) custom-call(bf16[64,512]{1,0:T(8,128)(2,1)} %x_loc.1, bf16[64,512]{1,0:T(8,128)(2,1)} %c_loc.1, ...), custom_call_target="tpu_custom_call" | custom-call | flops 14000000000 | bytes 21000000 | tf_op jit(solution)/shard_map/block_backward/pallas_call | solution.py:896
  129.7 4.2 %write_results.1 = (bf16[64,512]{1,0:T(8,128)(2,1)}, f32[4,512]{1,0:T(4,128)}, bf16[512,1152]{1,0:T(8,128)(2,1)}, bf16[1024,512]{1,0:T(8,128)(2,1)}, bf16[512,40...) custom-call(bf16[64,512]{1,0:T(8,128)(2,1)S(1)} %get-tuple-element.12.refs_0_, f32[4,512]{1,0:T(4,128)S(1)} %get-tuple-element.13.refs_1_, ...), custom_call_target="tpu_custom_call" | custom-call | tf_op jit(solution)/shard_map/write_results/pallas_call | solution.py:918

commit v6 on v5

--- a/solution.py
+++ b/solution.py
@@ -698,11 +698,12 @@
     use_act(0, 0)
     use_hid(0, 0)
 
+    gather_hid.go(0, 1, 2)
     heads.step_two()
-    gather_hid.go(0, 1, 2)
     pp_sum.step(2)
 
     gather_act.step_one()
+    near(use_act)
 
     heads.step_three()
     heads.step_four()
@@ -739,10 +740,8 @@
 
     loop(0, 4, early_body)
 
-    near(use_act)
-
+    gather_hid.step_one()
     gather_act.step_two()
-    gather_hid.step_one()
 
     near(use_hid)
     use_act(0, 2)

time: 134 us -> 131 us (0.978)
  Pallas kernels: 133 us -> 130 us
    pallas_call x1, Pallas kernels: 129 us -> 126 us  [on_device(): pl.pallas_call(kernel, out_shape=(pltpu.VMEM((ROWS, W), BF), pltpu.VMEM((...]
where the time goes in v6:
time: 131 us; the launch traced here: 130 us
  Pallas kernels  130 us (99%)
    pallas_call x1, Pallas kernels, on_device(): pl.pallas_call(kernel, out_shape=(pltpu.VMEM((ROWS, W), BF), pltpu.VMEM((...  126 us
    pallas_call x1, Pallas kernels, on_device(): pl.pallas_call(write_out, out_shape=tuple((jax.ShapeDtypeStruct(r.shape,...  4.21 us

profile of v6, /device:TPU:1, one launch (start us, length us, event | category | flops | bytes accessed | tf_op | source)
XLA Modules:
  0.0 130.4 jit_solution(10511702879273877481)
XLA Ops:
  0.6 125.6 %block_backward.1 = (bf16[64,512]{1,0:T(8,128)(2,1)S(1)}, f32[4,512]{1,0:T(4,128)S(1)}, bf16[512,1152]{1,0:T(8,128)(2,1)S(1)}, bf16[1024,512]{1,0:T(8,128)(2,1)S...) custom-call(bf16[64,512]{1,0:T(8,128)(2,1)} %x_loc.1, bf16[64,512]{1,0:T(8,128)(2,1)} %c_loc.1, ...), custom_call_target="tpu_custom_call" | custom-call | flops 14000000000 | bytes 21000000 | tf_op jit(solution)/shard_map/block_backward/pallas_call | solution.py:895
  126.2 4.2 %write_results.1 = (bf16[64,512]{1,0:T(8,128)(2,1)}, f32[4,512]{1,0:T(4,128)}, bf16[512,1152]{1,0:T(8,128)(2,1)}, bf16[1024,512]{1,0:T(8,128)(2,1)}, bf16[512,40...) custom-call(bf16[64,512]{1,0:T(8,128)(2,1)S(1)} %get-tuple-element.12.refs_0_, f32[4,512]{1,0:T(4,128)S(1)} %get-tuple-element.13.refs_1_, ...), custom_call_target="tpu_custom_call" | custom-call | tf_op jit(solution)/shard_map/write_results/pallas_call | solution.py:917
